TPU v7x, 256 devices: a whole 4x4x8 slice. The times are simulated.
256 devices in a mesh: freq: 4 (over x), src: 16 (over y_lo, z), rcv: 4 (over y_hi, core).
Axes of the slice: x: 4, y: 4 (y_hi: 2, y_lo: 2; y = y_hi * 2 + y_lo), z: 8, core: 2. Of those that a mesh axis runs over, the one named last changes fastest.
Arguments:
- direct: float32 [2048, 64, 1024], P(('rcv', 'src'), 'freq'), may hold values from -6 to 6
- reflection: float32 [2, 20, 2048, 2048], P(None, 'freq', 'src', 'rcv'), may hold values from -0.0390625 to 0.0390625
- onset_plus: int32 [2048, 64], P(('rcv', 'src'), 'freq'), may hold values from 256 to 1023
- onset_minus: int32 [2048, 64], P(('src', 'rcv'), 'freq'), may hold values from 256 to 1023
Outputs:
- focus_plus: float32 [2048, 64, 1024], P(('rcv', 'src'), 'freq')
- focus_minus: float32 [2048, 64, 1024], P(('src', 'rcv'), 'freq')
All inputs are finite; a program needn't handle non-finite values.
Results may differ from a plain program's by a relative error of at most 0.0001.
Values sent between devices are 32-bit elements; how exact they have to be, the bound alone decides.
A program may use at most 128 MiB of HBM per device.

v0:
```python
import math

import jax
import jax.numpy as jnp
from jax import lax
from jax.sharding import PartitionSpec as P

NF = 20
FIRST_BIN = 32
ITERS = 2


HIGHEST = lax.Precision.HIGHEST


def tables(length, lowest, bin_count):
    sample = jnp.arange(length, dtype=jnp.int32)
    orders = lowest + jnp.arange(bin_count, dtype=jnp.int32)
    phases = sample[:, None] * orders[None, :] % length
    angles = phases.astype(jnp.float32) * jnp.float32(2.0 * math.pi / length)
    factor = jnp.float32(math.sqrt(2.0 / length))
    return (factor * jnp.cos(angles), factor * jnp.sin(angles))


def window(onsets, length):
    sample = jnp.arange(length, dtype=jnp.int32)
    return (sample[None, None, :] < onsets[:, :, None]).astype(jnp.float32)


def to_spectrum(traces, cosine, sine_table):
    real_part = jnp.einsum("spt,tj->sjp", traces, cosine, precision=HIGHEST)
    imag_part = -jnp.einsum("spt,tj->sjp", traces, sine_table, precision=HIGHEST)
    return jnp.stack([real_part, imag_part], axis=2)


def to_time(spectrum, cosine, sine_table):
    return jnp.einsum("sjp,tj->spt", spectrum[:, :, 0], cosine, precision=HIGHEST) - jnp.einsum(
        "sjp,tj->spt", spectrum[:, :, 1], sine_table, precision=HIGHEST
    )


def combine_forward(first_term, second_term, half_width):
    real_out = first_term[..., :half_width] - second_term[..., half_width:]
    imag_out = first_term[..., half_width:] + second_term[..., :half_width]
    return jnp.concatenate([real_out, imag_out], axis=-1)


def combine_adjoint(first_term, second_term, half_width):
    real_out = first_term[..., :half_width] + second_term[..., half_width:]
    imag_out = first_term[..., half_width:] - second_term[..., :half_width]
    return jnp.concatenate([real_out, imag_out], axis=-1)


def per_device(direct, reflection, onset_plus, onset_minus):
    length = direct.shape[2]
    cosine, sine_table = tables(length, FIRST_BIN, NF)
    keep_plus = window(onset_plus, length)
    keep_minus = window(onset_minus, length)
    resp_real = reflection[0]
    resp_imag = reflection[1]
    half_width = direct.shape[1] * lax.axis_size("freq")
    bin_local = resp_real.shape[0]
    focus_plus = direct
    focus_minus = jnp.zeros((onset_minus.shape[0], onset_minus.shape[1], length), jnp.float32)
    for repeat in range(ITERS):
        spectrum = to_spectrum(focus_plus, cosine, sine_table)
        gathered = lax.all_gather(spectrum, "src", axis=0, tiled=True)
        regrouped = lax.all_to_all(gathered, "freq", split_axis=1, concat_axis=3, tiled=True)
        regrouped = regrouped.reshape(regrouped.shape[0], bin_local, 2 * half_width)
        first_term = jnp.einsum("jsr,rjq->sjq", resp_real, regrouped, precision=HIGHEST)
        second_term = jnp.einsum("jsr,rjq->sjq", resp_imag, regrouped, precision=HIGHEST)
        partial_value = combine_forward(first_term, second_term, half_width)
        summed = lax.psum_scatter(partial_value, "rcv", scatter_dimension=0, tiled=True)
        summed = summed.reshape(summed.shape[0], bin_local, 2, half_width)
        in_time = lax.all_to_all(summed, "freq", split_axis=3, concat_axis=1, tiled=True)
        focus_minus = keep_minus * to_time(in_time, cosine, sine_table)
        spectrum = to_spectrum(focus_minus, cosine, sine_table)
        regrouped = lax.all_to_all(spectrum, "freq", split_axis=1, concat_axis=3, tiled=True)
        regrouped = regrouped.reshape(regrouped.shape[0], bin_local, 2 * half_width)
        source_spec = lax.all_gather(regrouped, "rcv", axis=0, tiled=True)
        first_part = jnp.einsum("jsr,sjq->rjq", resp_real, source_spec, precision=HIGHEST)
        second_part = jnp.einsum("jsr,sjq->rjq", resp_imag, source_spec, precision=HIGHEST)
        update = lax.psum_scatter(
            combine_adjoint(first_part, second_part, half_width),
            "src",
            scatter_dimension=0,
            tiled=True,
        )
        update = update.reshape(update.shape[0], bin_local, 2, half_width)
        in_time = lax.all_to_all(update, "freq", split_axis=3, concat_axis=1, tiled=True)
        focus_plus = direct + keep_plus * to_time(in_time, cosine, sine_table)
    return (focus_plus, focus_minus)


def solution(mesh):
    in_specs = (
        P(("rcv", "src"), "freq", None),
        P(None, "freq", "src", "rcv"),
        P(("rcv", "src"), "freq"),
        P(("src", "rcv"), "freq"),
    )
    out_specs = (P(("rcv", "src"), "freq", None), P(("src", "rcv"), "freq", None))
    return jax.shard_map(
        per_device, mesh=mesh, in_specs=in_specs, out_specs=out_specs, check_vma=False
    )
```

profile of v0, /device:TPU:16, one launch (start us, length us, event | category | flops | bytes accessed | tf_op | source)
XLA Modules:
  0.0 660.6 jit_solution(7655723027584735323)
XLA Ops:
  7.2 6.9 %fusion.46 = f32[32,20,1,16]{0,1,3,2:T(8,128)S(1)} fusion(f32[32,16,1024]{2,1,0:T(8,128)} %param.4, s32[20]{0:T(128)S(1)} %iota_add_fusion), kind=kOutput, calls=%fused_computation.46 | convolution fusion | flops 126146560 | bytes 2138192 | tf_op jit(solution)/shard_map/spt,tj->sjp/dot_general | solution.py:32
  14.2 5.2 fusion.40
  19.4 1.3 copy.134
  20.8 103.6 %all-gather.3.cloned.1.call-done = f32[512,20,2,16]{1,3,2,0:T(8,128)} async-done(((f32[32,20,2,16]{1,3,2,0:T(8,128)}), f32[512,20,2,16]{1,3,2,0:T(8,128)}) %all-gather.3.cloned.1.call-update) | async-done | bytes 1310736 | tf_op jit(solution)/shard_map/all_gather | solution.py:67
  124.4 6.4 copy.135
  130.8 33.3 %all_to_all.132 = f32[512,20,2,16]{0,3,2,1:T(8,128)S(1)} all-to-all(f32[512,20,2,16]{0,3,2,1:T(8,128)} %copy.135), channel_id=1, replica_groups=mesh['freq'=4,'src'=16,'rcv'=4] {'freq'}, dimensions={1} | all-to-all | bytes 2621440 | tf_op jit(solution)/shard_map/all_to_all | solution.py:68
  164.2 1.4 fusion.34
  165.6 1.4 fusion.28
  167.0 1.0 copy.137
  168.0 27.3 %reduce-scatter.5.cloned.1.call-done = f32[32,5,128]{2,1,0:T(8,128)} async-done(((f32[128,5,128]{2,1,0:T(8,128)}), f32[32,5,128]{2,1,0:T(8,128)}) %reduce-scatter.5.cloned.1.call-update) | async-done | bytes 81936 | tf_op jit(solution)/shard_map/reduce_scatter | solution.py:73
  195.4 1.0 reshape.48
  196.7 1.0 reshape.52
  197.7 4.5 all-to-all-start.1
  202.2 5.6 all-to-all-done.1
  207.9 0.6 broadcast.136
  208.4 0.9 reduce
  210.1 2.2 fusion.94
  212.3 2.4 subtract_select_fusion.1
  214.7 5.2 fusion.55
  219.9 5.4 fusion.49
  225.7 8.1 %all_to_all.133 = f32[4,1,5120]{2,1,0:T(1,128)S(1)} all-to-all(f32[4,1,5120]{2,1,0:T(1,128)S(1)} %reshape.54), channel_id=1, replica_groups=mesh['freq'=4,'src'=16,'rcv'=4] {'freq'}, dimensions={0} | all-to-all | bytes 163840 | tf_op jit(solution)/shard_map/all_to_all | solution.py:78
  233.8 0.9 reduce.1
  234.9 7.6 %all_gather.13 = f32[128,5,128]{2,0,1:T(8,128)S(1)} all-gather(f32[32,5,128]{2,0,1:T(8,128)S(1)} %copy.148), channel_id=1, replica_groups=mesh['freq'=4,'src'=16,'rcv'=4] {'rcv'}, dimensions={0}, use_global_device_ids=true | all-gather | bytes 409600 | tf_op jit(solution)/shard_map/all_gather | solution.py:80
  242.6 1.3 convolution_bitcast_fusion.2
  243.9 1.3 convolution_bitcast_fusion.3
  245.5 1.2 pad_maximum_fusion
  246.6 2.7 copy.149
  249.4 73.9 %reduce-scatter.7.cloned.1.call-done = f32[32,5,128]{2,1,0:T(8,128)} async-done(((f32[512,5,128]{2,1,0:T(8,128)}), f32[32,5,128]{2,1,0:T(8,128)}) %reduce-scatter.7.cloned.1.call-update) | async-done | bytes 81936 | tf_op jit(solution)/shard_map/reduce_scatter | solution.py:83
  323.3 1.0 reshape.49
  324.6 1.0 reshape.56
  325.6 4.4 all-to-all-start.3
  330.6 5.2 all-to-all-done.3
  335.7 0.9 reduce.2
  337.4 2.2 fusion.91
  339.7 2.5 select_add_fusion.1
  342.2 5.2 fusion.64
  347.4 5.4 fusion.58
  352.9 1.3 copy.158
  354.2 95.5 %all-gather.5.cloned.1.call-done = f32[512,20,2,16]{1,3,2,0:T(8,128)} async-done(((f32[32,20,2,16]{1,3,2,0:T(8,128)}), f32[512,20,2,16]{1,3,2,0:T(8,128)}) %all-gather.5.cloned.1.call-update) | async-done | bytes 1310736 | tf_op jit(solution)/shard_map/all_gather | solution.py:67
  449.7 6.4 copy.159
  456.1 22.1 %all_to_all.134 = f32[512,20,2,16]{0,3,2,1:T(8,128)S(1)} all-to-all(f32[512,20,2,16]{0,3,2,1:T(8,128)} %copy.159), channel_id=1, replica_groups=mesh['freq'=4,'src'=16,'rcv'=4] {'freq'}, dimensions={1} | all-to-all | bytes 2621440 | tf_op jit(solution)/shard_map/all_to_all | solution.py:68
  478.4 1.4 fusion.37
  479.7 1.4 fusion.31
  481.2 1.0 copy.161
  482.3 27.3 %reduce-scatter.9.cloned.1.call-done = f32[32,5,128]{2,1,0:T(8,128)} async-done(((f32[128,5,128]{2,1,0:T(8,128)}), f32[32,5,128]{2,1,0:T(8,128)}) %reduce-scatter.9.cloned.1.call-update) | async-done | bytes 81936 | tf_op jit(solution)/shard_map/reduce_scatter | solution.py:73
  509.5 1.0 reshape.50
  511.2 10.0 %all_to_all.135 = f32[4,1,5120]{2,1,0:T(1,128)S(1)} all-to-all(f32[4,1,5120]{2,1,0:T(1,128)S(1)} %reshape.58), channel_id=1, replica_groups=mesh['freq'=4,'src'=16,'rcv'=4] {'freq'}, dimensions={0} | all-to-all | bytes 163840 | tf_op jit(solution)/shard_map/all_to_all | solution.py:75
  521.2 0.9 reduce.3
  522.9 2.2 fusion.88
  525.1 2.4 subtract_select_fusion
  527.4 5.2 fusion.73
  532.7 5.4 fusion.67
  538.4 8.1 %all_to_all.136 = f32[4,1,5120]{2,1,0:T(1,128)S(1)} all-to-all(f32[4,1,5120]{2,1,0:T(1,128)S(1)} %reshape.60), channel_id=1, replica_groups=mesh['freq'=4,'src'=16,'rcv'=4] {'freq'}, dimensions={0} | all-to-all | bytes 163840 | tf_op jit(solution)/shard_map/all_to_all | solution.py:78
  546.5 0.9 reduce.4
  547.7 7.6 %all_gather.15 = f32[128,5,128]{2,0,1:T(8,128)S(1)} all-gather(f32[32,5,128]{2,0,1:T(8,128)S(1)} %copy.172), channel_id=1, replica_groups=mesh['freq'=4,'src'=16,'rcv'=4] {'rcv'}, dimensions={0}, use_global_device_ids=true | all-gather | bytes 409600 | tf_op jit(solution)/shard_map/all_gather | solution.py:80
  555.3 1.3 convolution_bitcast_fusion
  556.6 1.3 convolution_bitcast_fusion.1
  558.3 1.8 copy.173
  560.1 74.0 %reduce-scatter.11.cloned.1.call-done = f32[32,5,128]{2,1,0:T(8,128)} async-done(((f32[512,5,128]{2,1,0:T(8,128)}), f32[32,5,128]{2,1,0:T(8,128)}) %reduce-scatter.11.cloned.1.call-update) | async-done | bytes 81936 | tf_op jit(solution)/shard_map/reduce_scatter | solution.py:83
  634.2 1.0 reshape.51
  635.8 9.8 %all_to_all.137 = f32[4,1,5120]{2,1,0:T(1,128)S(1)} all-to-all(f32[4,1,5120]{2,1,0:T(1,128)S(1)} %reshape.62), channel_id=1, replica_groups=mesh['freq'=4,'src'=16,'rcv'=4] {'freq'}, dimensions={0} | all-to-all | bytes 163840 | tf_op jit(solution)/shard_map/all_to_all | solution.py:90
  645.6 0.9 reduce.5
  647.3 2.2 fusion.85
  649.5 3.9 select_add_fusion
  (82 shorter events, 7.9 us)
Async XLA Ops:
  7.2 7.0 %copy-start.1 = (f32[32,16,1024]{2,1,0:T(8,128)S(1)}, f32[32,16,1024]{2,1,0:T(8,128)}, u32[]{:S(2)}) copy-start(f32[32,16,1024]{2,1,0:T(8,128)} %param.4) | copy-start | bytes 6291460
  7.2 117.2 %all-gather.3.cloned.1.call-start = ((), (), s32[]{:S(2)}) async-start(), calls=%async_computation.12 | async-start | bytes 8912896 | tf_op jit(solution)/shard_map/all_gather | solution.py:67
  20.7 174.6 %reduce-scatter.5.cloned.1.call-start = ((), (), s32[]{:S(2)}) async-start(), calls=%async_computation.13 | async-start | bytes 655360 | tf_op jit(solution)/shard_map/reduce_scatter | solution.py:73
  130.8 33.4 %copy-start = (f32[2,5,128,512]{3,2,1,0:T(8,128)S(1)}, f32[2,5,128,512]{3,2,1,0:T(8,128)}, u32[]{:S(2)}) copy-start(f32[2,5,128,512]{3,2,1,0:T(8,128)} %param.5) | copy-start | bytes 7864324
  166.9 35.2 %copy-start.5 = (s32[32,16]{0,1:T(8,128)S(1)}, s32[32,16]{0,1:T(8,128)}, u32[]{:S(2)}) copy-start(s32[32,16]{0,1:T(8,128)} %param.7) | copy-start | bytes 6148
  197.7 10.2 %all-to-all-start.1 = ((f32[4,1,5120]{2,1,0:T(1,128)}), f32[4,1,5120]{2,1,0:T(1,128)S(1)}, u32[]{:S(2)}, u32[]{:S(2)}) async-start(f32[4,1,5120]{2,1,0:T(1,128)} %reshape.52), calls=%async_computation.2 | async-start | bytes 163840 | tf_op jit(solution)/shard_map/all_to_all | solution.py:75
  202.1 121.2 %reduce-scatter.7.cloned.1.call-start = ((), (), s32[]{:S(2)}) async-start(), calls=%async_computation.14 | async-start | bytes 2228224 | tf_op jit(solution)/shard_map/reduce_scatter | solution.py:83
  249.4 81.1 %copy-start.6 = (s32[32,16]{0,1:T(8,128)S(1)}, s32[32,16]{0,1:T(8,128)}, u32[]{:S(2)}) copy-start(s32[32,16]{0,1:T(8,128)} %param.6) | copy-start | bytes 6148
  325.6 10.1 %all-to-all-start.3 = ((f32[4,1,5120]{2,1,0:T(1,128)}), f32[4,1,5120]{2,1,0:T(1,128)S(1)}, u32[]{:S(2)}, u32[]{:S(2)}) async-start(f32[4,1,5120]{2,1,0:T(1,128)} %reshape.56), calls=%async_computation.5 | async-start | bytes 163840 | tf_op jit(solution)/shard_map/all_to_all | solution.py:90
  330.0 119.7 %all-gather.5.cloned.1.call-start = ((), (), s32[]{:S(2)}) async-start(), calls=%async_computation.15 | async-start | bytes 8912896 | tf_op jit(solution)/shard_map/all_gather | solution.py:67
  337.4 2.2 copy-start.2
  354.2 155.3 %reduce-scatter.9.cloned.1.call-start = ((), (), s32[]{:S(2)}) async-start(), calls=%async_computation.16 | async-start | bytes 655360 | tf_op jit(solution)/shard_map/reduce_scatter | solution.py:73
  482.2 151.9 %reduce-scatter.11.cloned.1.call-start = ((), (), s32[]{:S(2)}) async-start(), calls=%async_computation.17 | async-start | bytes 2228224 | tf_op jit(solution)/shard_map/reduce_scatter | solution.py:83
  527.4 10.7 %copy-start.4 = (f32[32,16,1024]{2,1,0:T(8,128)}, f32[32,16,1024]{2,1,0:T(8,128)S(1)}, u32[]{:S(2)}) copy-start(f32[32,16,1024]{2,1,0:T(8,128)S(1)} %subtract_select_fusion) | copy-start | bytes 6291460
  646.8 2.7 copy-start.3
Sparse Core Ops, SparseCore 0:
  20.9 103.4 all-gather.2
  168.2 27.1 reduce-scatter.4
  249.5 73.7 reduce-scatter.6
  354.3 95.3 all-gather.4
  482.3 27.1 reduce-scatter.8
  560.3 73.8 reduce-scatter.10
where the time goes:
time: 668 us; the launch traced here: 661 us
  waiting for transfers between devices  413 us (62%)
  blocking collectives  107 us (16%)
  matrix products  74.6 us (11%)
  local copies, waits for them, and re-layouts  34.7 us (5%)
  between operations  15.2 us (2%)
  starting transfers between devices  9.51 us (1%)
  other arithmetic  7.39 us (1%)
    all_gather x2, waiting for transfers between devices, per_device(): gathered = lax.all_gather(spectrum, 'src', axis=0, tiled=True)  199 us
    reduce_scatter x2, waiting for transfers between devices, per_device(): lax.psum_scatter(combine_adjoint(first_part, second_part, half_width), 's...  148 us
    all_to_all x2, blocking collectives, per_device(): lax.all_to_all(gathered, 'freq', split_axis=1, concat_axis=3, tiled=True)  55.4 us
    reduce_scatter x2, waiting for transfers between devices, per_device(): lax.psum_scatter(partial_value, 'rcv', scatter_dimension=0, tiled=True)  54.6 us
    dot_general x4, matrix products, to_spectrum(): jnp.einsum('spt,tj->sjp', traces, sine_table, precision=HIGHEST)  22.6 us
    dot_general x4, matrix products, to_spectrum(): real_part = jnp.einsum('spt,tj->sjp', traces, cosine, precision=HIGHEST)  21.5 us
    all_to_all x2, blocking collectives, per_device(): lax.all_to_all(spectrum, 'freq', split_axis=1, concat_axis=3, tiled=True)  16.2 us
    all_gather x2, blocking collectives, per_device(): source_spec = lax.all_gather(regrouped, 'rcv', axis=0, tiled=True)  15.3 us
  transfers between devices with their start and end apart: 8, of which 8 were waited for; matrix products, arithmetic and copies ran while one was open for 0% of the time, Pallas kernels for 0%

commit v1 on v0

v1 whole, which is shorter than its diff:
```python
import math

import jax
import jax.numpy as jnp
import ml_dtypes
import numpy as np
from jax import lax
from jax.experimental import pallas as pl
from jax.experimental.pallas import tpu as pltpu
from jax.sharding import PartitionSpec as P

FIRST_BIN = 32
ITERS = 2
MESH = pl.DeviceIdType.MESH

NF = 20
NX = 4
BL = NF // NX
FP = 16
ST = 32
NT = 1024
NZ = 8
LN = 128
SRC = 128
RCV = 512
ZA = 3
COLS = 2 * NF
WIDE = COLS * FP
STEP = 8
ROWS = STEP * FP


def tables():
    k = (np.arange(NT)[:, None] * (FIRST_BIN + np.arange(NF))[None, :]) % NT
    angle = 2.0 * math.pi * k / NT
    scale = math.sqrt(2.0 / NT)
    table = np.stack([scale * np.cos(angle), -scale * np.sin(angle)], axis=2)
    table = table.reshape(NT, COLS).astype(np.float32)
    high = table.astype(ml_dtypes.bfloat16).astype(np.float32)
    low = (table - high).astype(ml_dtypes.bfloat16).astype(np.float32)
    into = np.zeros((2, NT, LN), np.float32)
    into[0, :, :COLS] = high
    into[0, :, COLS : 2 * COLS] = low
    into[1, :, :COLS] = high
    back = np.zeros((LN, NT), np.float32)
    back[:COLS] = high.T
    back[COLS : 2 * COLS] = high.T
    back[2 * COLS : 3 * COLS] = low.T
    spread = np.zeros((LN, WIDE), np.float32)
    collect = np.zeros((2, WIDE, LN), np.float32)
    for b in range(NF):
        for c in range(2):
            for p in range(FP):
                f, j = b // BL, b % BL
                lane = (f * LN + j * 32 if j < 4 else 4 * LN + f * 32) + c * FP + p
                col = 2 * b + c
                spread[col, lane] = 1
                spread[COLS + col, lane] = 1
                collect[0, lane, col] = 1
                collect[0, lane, 2 * COLS + col] = 1
                collect[1, lane, COLS + col] = 1
    return [a.astype(ml_dtypes.bfloat16) for a in (into, spread, collect, back)]


def halves(x):
    high = x.astype(jnp.bfloat16)
    return high, (x - high.astype(jnp.float32)).astype(jnp.bfloat16)


def mm(a, b):
    return lax.dot_general(a, b, (((1,), (0,)), ((), ())), preferred_element_type=jnp.float32)


def turn(x, lanes):
    lanes = lanes % LN
    return x if lanes == 0 else pltpu.roll(x, lanes, 1)


def pick(parts, i):
    group = lax.broadcasted_iota(jnp.int32, parts[0].shape, 1) // 32
    out = turn(parts[0], -i * 32)
    for k in range(1, 4):
        out = jnp.where(group == k, turn(parts[k], (k - i) * 32), out)
    return out


def own_focus():
    row = lax.broadcasted_iota(jnp.int32, (ROWS, WIDE), 0) % FP
    lane = lax.broadcasted_iota(jnp.int32, (ROWS, WIDE), 1) % FP
    return row == lane


def to_spectrum(x, into, spread):
    high, low = halves(x)
    s = mm(high, into[0]) + mm(low, into[1])
    high, low = halves(s)
    e = mm(high, spread[...]) + mm(low, spread[...])
    e = jnp.where(own_focus(), e, 0.0).reshape(STEP, FP, WIDE)
    return jnp.sum(e, axis=1)


def to_time(z, collect, back):
    high = z.astype(jnp.bfloat16).astype(jnp.float32)
    low = z - high
    own = own_focus()

    def rows(v):
        v = jnp.broadcast_to(v[:, None, :], (STEP, FP, WIDE)).reshape(ROWS, WIDE)
        return jnp.where(own, v, 0.0).astype(jnp.bfloat16)

    g = mm(rows(high), collect[0]) + mm(rows(low), collect[1])
    return mm(g.astype(jnp.bfloat16), back[...])


def is_real(shape):
    return lax.broadcasted_iota(jnp.int32, shape, 1) % 32 < FP


def swap_parts(x, real):
    return jnp.where(real, turn(x, -FP), turn(x, FP))


def kernel(
    direct, refl, on_plus, on_minus, into, spread, collect, back,
    out_plus, out_minus,
    r_high, r_low, t_high, t_low, onset, spec, piece, landed,
    xs, y, r4a, r4b, cs, h, rsy, rsz, rsp, rsf, send_sem, recv_sem,
):
    f = lax.axis_index("freq")
    src = lax.axis_index("src")
    rcv = lax.axis_index("rcv")
    line = src // NZ
    z = src % NZ
    high_y = rcv // 2
    core = rcv % 2
    right = (f, line * NZ + (z + 1) % NZ, rcv)
    left = (f, line * NZ + (z + NZ - 1) % NZ, rcv)
    across = (f, (1 - line) * NZ + z, rcv)
    sibling = (f, src, high_y * 2 + 1 - core)
    opposite = (f, src, (1 - high_y) * 2 + core)
    freqs = [None] + [(f + o) % NX for o in range(1, NX)]
    peers = [right, left, across, sibling, opposite] + [(q, src, rcv) for q in freqs[1:]]

    barrier = pltpu.get_barrier_semaphore()
    for peer in peers:
        pl.semaphore_signal(barrier, inc=1, device_id=peer, device_id_type=MESH)

    names = {}

    def copy(name, source, target, device):
        n = names.setdefault(name, len(names))
        return pltpu.make_async_remote_copy(
            src_ref=source, dst_ref=target, send_sem=send_sem.at[n], recv_sem=recv_sem.at[n],
            device_id=device, device_id_type=MESH,
        )

    def rows_at(on_line, dist):
        block = on_line * NZ + (z + dist + NZ) % NZ
        return pl.ds(pl.multiple_of(block * ST, ST), ST)

    def half_at(on_line, dist, part):
        block = on_line * NZ + (z + dist + NZ) % NZ
        return pl.ds(pl.multiple_of(block * ST + part * (ST // 2), ST // 2), ST // 2)

    def rcv_rows(hy, c):
        return pl.ds(pl.multiple_of((hy * 2 + c) * ST, ST), ST)

    def prepare(j, _):
        block = refl[:, j].reshape(2 * SRC, RCV)
        high, low = halves(block)
        r_high[j] = high
        r_low[j] = low
        high, low = halves(block.T)
        t_high[j] = high
        t_low[j] = low
        return 0

    lax.fori_loop(0, BL, prepare, 0)
    eye = (
        lax.broadcasted_iota(jnp.int32, (ST, FP, FP), 1)
        == lax.broadcasted_iota(jnp.int32, (ST, FP, FP), 2)
    )
    for k, on in ((0, on_plus), (1, on_minus)):
        v = jnp.broadcast_to(on[...].astype(jnp.float32)[:, None, :], (ST, FP, FP))
        v = jnp.sum(jnp.where(eye, v, 0.0), axis=2, keepdims=True)
        onset[k] = jnp.broadcast_to(v.reshape(ST * FP, 1), (ST * FP, LN))

    def first(i, _):
        at = pl.ds(pl.multiple_of(i * STEP, STEP), STEP)
        spec[at] = to_spectrum(direct[at].reshape(ROWS, NT), into, spread)
        return 0

    lax.fori_loop(0, ST // STEP, first, 0)
    pl.semaphore_wait(barrier, len(peers))

    def pack_spec(ph):
        last = spec[:, 4 * LN :]
        parts = [last[8 * b : 8 * b + 8] for b in range(4)]
        for q in range(NX):
            piece[ph, q, 0:ST] = spec[:, q * LN : (q + 1) * LN]
            piece[ph, q, ST : ST + 8] = pick(parts, q)

    def pack_bins(ph, blocks):
        parts = [blocks[4][8 * b : 8 * b + 8] for b in range(4)]
        for q in range(NX):
            piece[ph, q, 0:ST] = pick(blocks[:4], q)
            piece[ph, q, ST : ST + 8] = pick(parts, q)

    def exchange(ph):
        sent = []
        for o in (2, 1, 3):
            c = copy(("x", ph, o), piece.at[ph, freqs[o]], landed.at[ph, f], (freqs[o], src, rcv))
            c.start()
            sent.append(c)
        landed[ph, f] = piece[ph, f]
        for c in sent:
            c.wait()

    def take_spec(ph):
        for q in range(NX):
            spec[:, q * LN : (q + 1) * LN] = landed[ph, q, 0:ST]
        parts = [landed[ph, q, ST : ST + 8] for q in range(NX)]
        for b in range(4):
            spec[8 * b : 8 * b + 8, 4 * LN :] = pick(parts, b)

    def take_bins(ph):
        whole = [landed[ph, q, 0:ST] for q in range(NX)]
        parts = [landed[ph, q, ST : ST + 8] for q in range(NX)]
        out = [pick(whole, j) for j in range(4)]
        out.append(jnp.concatenate([pick(parts, b) for b in range(4)], axis=0))
        return out

    other = 1 - line
    own_rows = rows_at(line, 0)
    my_chunk = rcv_rows(high_y, core)
    opp_chunk = rcv_rows(1 - high_y, core)

    def gather_sources():
        pending = []

        def go(name, bins, at, device):
            c = copy(name, xs.at[bins, at], xs.at[bins, at], device)
            c.start()
            pending.append(c)
            return c

        whole, low, top = slice(0, BL), slice(0, ZA), slice(ZA, BL)
        cross = go(("gy", 0, 1), top, own_rows, across)
        cross_all = [go(("gy", 0, 0), low, own_rows, across)]
        ways = ((0, 1, right), (1, -1, left))
        moving = [None, None]
        moving_other = [None, None]
        for w, sign, dev in ways:
            moving[w] = go(("gz", w, 1), whole, own_rows, dev)
        cross.wait_recv()
        for w, sign, dev in ways:
            moving_other[w] = go(("gp", w, 1), top, rows_at(other, 0), dev)
        for hop in range(1, 4):
            for w, sign, dev in ways:
                moving[w].wait_recv()
                dist = -sign * hop
                at = rows_at(line, dist) if hop < 3 else half_at(line, dist, w)
                full = rows_at(line, dist)
                moving[w] = go(("gz", w, hop + 1), whole, at, dev)
                cross_all.append(go(("gy", dist, 0), low, full, across))
            for w, sign, dev in ways:
                moving_other[w].wait_recv()
                dist = -sign * hop
                at = rows_at(other, dist) if hop < 3 else half_at(other, dist, w)
                moving_other[w] = go(("gp", w, hop + 1), top, at, dev)
        for w in (0, 1):
            moving[w].wait_recv()
        cross_all.append(go(("gy", 4, 0), low, rows_at(line, 4), across))
        for w in (0, 1):
            moving_other[w].wait_recv()
        for c in cross_all:
            c.wait_recv()
        for c in pending:
            c.wait_send()

    def scatter_receivers():
        whole, low, top = slice(0, BL), slice(0, ZA), slice(ZA, BL)
        pending = []

        def go(name, source, target, device):
            c = copy(name, source, target, device)
            c.start()
            pending.append(c)
            return c

        cross = {}
        for dist in (4, 3, -3, 2, -2, 1, -1, 0):
            cross[dist] = go(
                ("sy", dist), h.at[low, rows_at(other, dist)], rsy.at[:, dist + 3], across
            )
        ways = ((0, 1, right), (1, -1, left))
        moving = [None, None]
        moving_other = [None, None]
        for w, sign, dev in ways:
            at = half_at(other, 4, w)
            moving_other[w] = go(
                ("sp", w, 4), h.at[top, at], rsp.at[w, 3, :, pl.ds(w * (ST // 2), ST // 2)], dev
            )
        cross[4].wait_recv()
        at = rows_at(line, 4)
        h[low, at] = h[low, at] + rsy[:, 7]
        for w, sign, dev in ways:
            at = half_at(line, 4, w)
            moving[w] = go(
                ("sz", w, 4), h.at[whole, at], rsz.at[w, 3, :, pl.ds(w * (ST // 2), ST // 2)], dev
            )
        for hop in (3, 2, 1):
            for w, sign, dev in ways:
                dist = sign * hop
                at = rows_at(line, dist)
                oat = rows_at(other, dist)
                cross[dist].wait_recv()
                h[low, at] = h[low, at] + rsy[:, dist + 3]
                moving[w].wait_recv()
                moving_other[w].wait_recv()
                if hop == 3:
                    part = slice(w * (ST // 2), (w + 1) * (ST // 2))
                    half = half_at(line, dist, w)
                    ohalf = half_at(other, dist, w)
                    h[:, half] = h[:, half] + rsz[w, 3, :, part]
                    h[top, ohalf] = h[top, ohalf] + rsp[w, 3, :, part]
                else:
                    h[:, at] = h[:, at] + rsz[w, hop]
                    h[top, oat] = h[top, oat] + rsp[w, hop]
                moving[w] = go(("sz", w, hop), h.at[whole, at], rsz.at[w, hop - 1], dev)
                moving_other[w] = go(("sp", w, hop), h.at[top, oat], rsp.at[w, hop - 1], dev)
        oat = rows_at(other, 0)
        for w in (0, 1):
            moving_other[w].wait_recv()
        h[top, oat] = h[top, oat] + rsp[0, 0] + rsp[1, 0]
        last = go(("sf", 0), h.at[top, oat], rsf, across)
        cross[0].wait_recv()
        h[low, own_rows] = h[low, own_rows] + rsy[:, 3]
        for w in (0, 1):
            moving[w].wait_recv()
        h[:, own_rows] = h[:, own_rows] + rsz[0, 0] + rsz[1, 0]
        last.wait_recv()
        h[top, own_rows] = h[top, own_rows] + rsf[...]
        for c in pending:
            c.wait_send()

    def iterate(it, _):
        pack_spec(0)
        exchange(0)
        for j, block in enumerate(take_bins(0)):
            xs[j, own_rows] = block
        gather_sources()

        def forward(j, _):
            x_high, x_low = halves(xs[j])
            both = mm(r_high[j], jnp.concatenate([x_high, x_low], axis=1))
            g = both[:, :LN] + both[:, LN:] + mm(r_low[j], x_high)
            real = is_real((SRC, LN))
            turned = swap_parts(g[SRC:], real)
            y[j] = g[:SRC] + jnp.where(real, -turned, turned)
            return 0

        lax.fori_loop(0, BL, forward, 0)

        sib = 1 - core
        a = copy(("ra", 0), y.at[:, rcv_rows(1 - high_y, sib)], r4a.at[0], sibling)
        a.start()
        b = copy(("ra", 1), y.at[:, rcv_rows(high_y, sib)], r4a.at[1], sibling)
        b.start()
        a.wait_recv()
        y[:, opp_chunk] = y[:, opp_chunk] + r4a[0]
        c = copy(("rb", 0), y.at[:, opp_chunk], r4b, opposite)
        c.start()
        b.wait_recv()
        y[:, my_chunk] = y[:, my_chunk] + r4a[1]
        c.wait_recv()
        total = y[:, my_chunk] + r4b[...]
        pack_bins(1, [total[j] for j in range(BL)])
        for d in (a, b, c):
            d.wait_send()
        exchange(1)
        take_spec(1)

        def up(i, _):
            at = pl.ds(pl.multiple_of(i * STEP, STEP), STEP)
            rows = pl.ds(pl.multiple_of(i * ROWS, ROWS), ROWS)
            t = lax.broadcasted_iota(jnp.int32, (ROWS, NT), 1).astype(jnp.float32)
            x = to_time(spec[at], collect, back)
            x = jnp.where(t < onset[1, rows, 0:1], x, 0.0)
            out_minus[at] = x.reshape(STEP, FP, NT)
            spec[at] = to_spectrum(x, into, spread)
            return 0

        lax.fori_loop(0, ST // STEP, up, 0)
        pack_spec(2)
        exchange(2)
        for j, block in enumerate(take_bins(2)):
            cs[j, my_chunk] = block
        a = copy(("ca", 0), cs.at[:, my_chunk], cs.at[:, my_chunk], opposite)
        a.start()
        b = copy(("ca", 1), cs.at[:, my_chunk], cs.at[:, my_chunk], sibling)
        b.start()
        a.wait_recv()
        c = copy(("ca", 2), cs.at[:, opp_chunk], cs.at[:, opp_chunk], sibling)
        c.start()
        b.wait_recv()
        c.wait_recv()
        for d in (a, b, c):
            d.wait_send()

        def adjoint(j, _):
            real = is_real((SRC, LN))
            block = cs[j]
            turned = swap_parts(block, real)
            stacked = jnp.concatenate([block, jnp.where(real, turned, -turned)], axis=0)
            c_high, c_low = halves(stacked)
            both = mm(t_high[j], jnp.concatenate([c_high, c_low], axis=1))
            h[j] = both[:, :LN] + both[:, LN:] + mm(t_low[j], c_high)
            return 0

        lax.fori_loop(0, BL, adjoint, 0)
        scatter_receivers()
        pack_bins(3, [h[j, own_rows] for j in range(BL)])
        exchange(3)
        take_spec(3)

        def down(i, _):
            at = pl.ds(pl.multiple_of(i * STEP, STEP), STEP)
            rows = pl.ds(pl.multiple_of(i * ROWS, ROWS), ROWS)
            t = lax.broadcasted_iota(jnp.int32, (ROWS, NT), 1).astype(jnp.float32)
            x = to_time(spec[at], collect, back)
            x = direct[at].reshape(ROWS, NT) + jnp.where(t < onset[0, rows, 0:1], x, 0.0)
            out_plus[at] = x.reshape(STEP, FP, NT)

            @pl.when(it < ITERS - 1)
            def _():
                spec[at] = to_spectrum(x, into, spread)

            return 0

        lax.fori_loop(0, ST // STEP, down, 0)
        return 0

    lax.fori_loop(0, ITERS, iterate, 0)


MESSAGES = 96


def per_device(direct, reflection, onset_plus, onset_minus):
    vmem = pl.BlockSpec(memory_space=pltpu.VMEM)
    f32, bf16 = jnp.float32, jnp.bfloat16
    traces = jax.ShapeDtypeStruct((ST, FP, NT), f32)
    return pl.pallas_call(
        kernel,
        out_shape=(traces, traces),
        in_specs=[vmem] * 8,
        out_specs=(vmem, vmem),
        scratch_shapes=[
            pltpu.VMEM((BL, 2 * SRC, RCV), bf16),
            pltpu.VMEM((BL, 2 * SRC, RCV), bf16),
            pltpu.VMEM((BL, RCV, 2 * SRC), bf16),
            pltpu.VMEM((BL, RCV, 2 * SRC), bf16),
            pltpu.VMEM((2, ST * FP, LN), f32),
            pltpu.VMEM((ST, WIDE), f32),
            pltpu.VMEM((4, NX, ST + 8, LN), f32),
            pltpu.VMEM((4, NX, ST + 8, LN), f32),
            pltpu.VMEM((BL, RCV, LN), f32),
            pltpu.VMEM((BL, SRC, LN), f32),
            pltpu.VMEM((2, BL, ST, LN), f32),
            pltpu.VMEM((BL, ST, LN), f32),
            pltpu.VMEM((BL, SRC, LN), f32),
            pltpu.VMEM((BL, RCV, LN), f32),
            pltpu.VMEM((ZA, NZ, ST, LN), f32),
            pltpu.VMEM((2, 4, BL, ST, LN), f32),
            pltpu.VMEM((2, 4, BL - ZA, ST, LN), f32),
            pltpu.VMEM((BL - ZA, ST, LN), f32),
            pltpu.SemaphoreType.DMA((MESSAGES,)),
            pltpu.SemaphoreType.DMA((MESSAGES,)),
        ],
        compiler_params=pltpu.CompilerParams(
            collective_id=0, has_side_effects=True, vmem_limit_bytes=56 * 1024 * 1024
        ),
    )(direct, reflection, onset_plus, onset_minus, *[jnp.asarray(a) for a in tables()])


def solution(mesh):
    in_specs = (
        P(("rcv", "src"), "freq", None),
        P(None, "freq", "src", "rcv"),
        P(("rcv", "src"), "freq"),
        P(("src", "rcv"), "freq"),
    )
    out_specs = (P(("rcv", "src"), "freq", None), P(("src", "rcv"), "freq", None))
    return jax.shard_map(
        per_device, mesh=mesh, in_specs=in_specs, out_specs=out_specs, check_vma=False
    )
```

time: 668 us -> 177 us (0.26)
  waiting for transfers between devices: 413 us -> 0 us
  Pallas kernels: 0 us -> 168 us
  blocking collectives: 107 us -> 0 us
  matrix products: 74.6 us -> 0 us
  local copies, waits for them, and re-layouts: 34.7 us -> 7.38 us
  between operations: 15.2 us -> 0.65 us
  starting transfers between devices: 9.51 us -> 0 us
  other arithmetic: 7.39 us -> 0 us
    reduce_scatter x4 -> x0, waiting for transfers between devices: 203 us -> none  [the longest x2 148 us: per_device(): lax.psum_scatter(combine_adjoint(first_part, second_part, half_width), 's...]
    all_gather x2 -> x0, waiting for transfers between devices: 199 us -> none  [per_device(): gathered = lax.all_gather(spectrum, 'src', axis=0, tiled=True)]
    pallas_call x0 -> x1, Pallas kernels: none -> 168 us  [per_device(): pl.pallas_call(kernel, out_shape=(traces, traces), in_specs=[vmem] * 8, o...]
    all_to_all x6 -> x0, blocking collectives: 91.4 us -> none  [the longest x2 55.4 us: per_device(): lax.all_to_all(gathered, 'freq', split_axis=1, concat_axis=3, tiled=True)]
    dot_general x24 -> x0, matrix products: 74.6 us -> none  [the longest x4 22.6 us: to_spectrum(): jnp.einsum('spt,tj->sjp', traces, sine_table, precision=HIGHEST)]
    all_gather x2 -> x0, blocking collectives: 15.3 us -> none  [per_device(): source_spec = lax.all_gather(regrouped, 'rcv', axis=0, tiled=True)]
    all_gather x2 -> x0, local copies, waits for them, and re-layouts: 12.7 us -> none  [per_device(): gathered = lax.all_gather(spectrum, 'src', axis=0, tiled=True)]
    all_to_all x2 -> x0, waiting for transfers between devices: 10.8 us -> none  [the longest x1 5.63 us: per_device(): lax.all_to_all(summed, 'freq', split_axis=3, concat_axis=1, tiled=True)]
  transfers between devices with their start and end apart: 8 -> 0, of which waited for: 8 -> 0; matrix products, arithmetic and copies ran while one was open for 0% -> 0% of each run, Pallas kernels for 0% -> 0%
where the time goes in v1:
time: 177 us; the launch traced here: 176 us
  Pallas kernels  168 us (95%)
  local copies, waits for them, and re-layouts  7.38 us (4%)
    pallas_call x1, Pallas kernels, per_device(): pl.pallas_call(kernel, out_shape=(traces, traces), in_specs=[vmem] * 8, o...  168 us
    unnamed x6, local copies, waits for them, and re-layouts  7.38 us

profile of v1, /device:TPU:16, one launch (start us, length us, event | category | flops | bytes accessed | tf_op | source)
XLA Modules:
  0.0 176.0 jit_solution(8058521251233678897)
XLA Ops:
  0.6 1.4 copy.10.on_plus
  2.0 1.4 copy.11.on_minus
  3.4 168.0 %shard_map.95 = (f32[32,16,1024]{2,1,0:T(8,128)}, f32[32,16,1024]{2,1,0:T(8,128)}) custom-call(f32[32,16,1024]{2,1,0:T(8,128)} %direct.1, f32[2,5,128,512]{3,2,1,0:T(8,128)} %refl.1, s32[32,16]{1,0:T(8,128)} %copy.10.on_plus, s32[32,16]{1,0:T(8,128)} %copy.11.on_minus, bf16[2,1024,128]{2,1,0:T(8,128)(2,1)} %constant.8.clone.into, ...), custom_call_target="tpu_custom_call" | custom-call | tf_op jit(solution)/shard_map/pallas_call | solution.py:454
  171.4 0.0 copy-start
  171.4 3.3 %copy.14 = f32[32,16,1024]{2,1,0:T(8,128)} copy(f32[32,16,1024]{2,1,0:T(8,128)} %get-tuple-element.4) | data formatting | bytes 4194304
  174.7 0.0 copy-done
  174.7 1.3 copy.15
Async XLA Ops:
  171.4 3.3 %copy-start = (f32[32,16,1024]{2,1,0:T(8,128)S(1)}, f32[32,16,1024]{2,1,0:T(8,128)}, u32[]{:S(2)}) copy-start(f32[32,16,1024]{2,1,0:T(8,128)} %get-tuple-element.5) | copy-start | bytes 6291460

commit v2 on v0

v2 whole, which is shorter than its diff:
```python
import math

import jax
import jax.numpy as jnp
import ml_dtypes
import numpy as np
from jax import lax
from jax.experimental import pallas as pl
from jax.experimental.pallas import tpu as pltpu
from jax.sharding import PartitionSpec as P

FIRST_BIN = 32
ITERS = 2
MESH = pl.DeviceIdType.MESH

NF = 20
NX = 4
BL = NF // NX
FP = 16
GROUPS = 2
SH = GROUPS
PG = FP // GROUPS
ST = 32 // SH
NT = 1024
NZ = 8
LN = 128
SRC = 128
RCV = 512
NS = 16
NR = 4
PR = ST + 8
COLS = 2 * NF
WIDE = COLS * FP
STEP = 8
ROWS = STEP * FP


def tables():
    k = (np.arange(NT)[:, None] * (FIRST_BIN + np.arange(NF))[None, :]) % NT
    angle = 2.0 * math.pi * k / NT
    scale = math.sqrt(2.0 / NT)
    table = np.stack([scale * np.cos(angle), -scale * np.sin(angle)], axis=2)
    table = table.reshape(NT, COLS).astype(np.float32)
    high = table.astype(ml_dtypes.bfloat16).astype(np.float32)
    low = (table - high).astype(ml_dtypes.bfloat16).astype(np.float32)
    into = np.zeros((2, NT, LN), np.float32)
    into[0, :, :COLS] = high
    into[0, :, COLS : 2 * COLS] = low
    into[1, :, :COLS] = high
    back = np.zeros((LN, NT), np.float32)
    back[:COLS] = high.T
    back[COLS : 2 * COLS] = high.T
    back[2 * COLS : 3 * COLS] = low.T
    spread = np.zeros((LN, WIDE), np.float32)
    collect = np.zeros((2, WIDE, LN), np.float32)
    for b in range(NF):
        for c in range(2):
            for p in range(FP):
                f, j = b // BL, b % BL
                lane = (f * LN + j * 32 if j < 4 else 4 * LN + f * 32) + c * FP + p
                col = 2 * b + c
                spread[col, lane] = 1
                spread[COLS + col, lane] = 1
                collect[0, lane, col] = 1
                collect[0, lane, 2 * COLS + col] = 1
                collect[1, lane, COLS + col] = 1
    return [a.astype(ml_dtypes.bfloat16) for a in (into, spread, collect, back)]


def halves(x):
    high = x.astype(jnp.bfloat16)
    return high, (x - high.astype(jnp.float32)).astype(jnp.bfloat16)


def mm(a, b):
    return lax.dot_general(a, b, (((1,), (0,)), ((), ())), preferred_element_type=jnp.float32)


def turn(x, lanes):
    lanes = lanes % LN
    return x if lanes == 0 else pltpu.roll(x, lanes, 1)


def pick(parts, i):
    group = lax.broadcasted_iota(jnp.int32, parts[0].shape, 1) // 32
    out = turn(parts[0], -i * 32)
    for k in range(1, len(parts)):
        out = jnp.where(group == k, turn(parts[k], (k - i) * 32), out)
    return out


def own_focus():
    row = lax.broadcasted_iota(jnp.int32, (ROWS, WIDE), 0) % FP
    lane = lax.broadcasted_iota(jnp.int32, (ROWS, WIDE), 1) % FP
    return row == lane


def to_spectrum(x, into, spread):
    high, low = halves(x)
    s = mm(high, into[0]) + mm(low, into[1])
    high, low = halves(s)
    e = mm(high, spread[...]) + mm(low, spread[...])
    e = jnp.where(own_focus(), e, 0.0).reshape(STEP, FP, WIDE)
    return jnp.sum(e, axis=1)


def to_time(z, collect, back):
    high = z.astype(jnp.bfloat16).astype(jnp.float32)
    low = z - high
    own = own_focus()

    def rows(v):
        v = jnp.broadcast_to(v[:, None, :], (STEP, FP, WIDE)).reshape(ROWS, WIDE)
        return jnp.where(own, v, 0.0).astype(jnp.bfloat16)

    g = mm(rows(high), collect[0]) + mm(rows(low), collect[1])
    return mm(g.astype(jnp.bfloat16), back[...])


def is_real(shape):
    return lax.broadcasted_iota(jnp.int32, shape, 1) % 32 < FP


def swap_parts(x, real):
    return jnp.where(real, turn(x, -FP), turn(x, FP))


def lane_block(shape):
    return lax.broadcasted_iota(jnp.int32, shape, 1) // PG % SH


def unfold(x):
    if SH == 1:
        return x
    at = lane_block(x.shape)
    return jnp.concatenate(
        [jnp.where(at == 0, x, turn(x, PG)), jnp.where(at == 1, x, turn(x, -PG))], axis=0
    )


def fold(x):
    if SH == 1:
        return x
    n = x.shape[0] // 2
    return jnp.where(lane_block((n, LN)) == 0, x[:n], x[n:])


def reorder(x, outer, inner):
    if SH == 1:
        return x
    return jnp.concatenate(
        [x[(o * SH + s) * inner : (o * SH + s + 1) * inner] for s in range(SH) for o in range(outer)],
        axis=0,
    )


def kernel(
    direct, refl, on_plus, on_minus, into, spread, collect, back,
    out_plus, out_minus,
    r_high, r_low, t_high, t_low, onset, spec, piece, piece_sum, land_g, land_r, land_f, land_s,
    xs, y, r4a, cs, h, rs, send_sem, recv_sem,
):
    f = lax.axis_index("freq")
    src = lax.axis_index("src")
    rcv = lax.axis_index("rcv")
    line = src // NZ
    z = src % NZ
    other = 1 - line
    high_y = rcv // 2
    core = rcv % 2
    freqs = [f] + [(f + o) % NX for o in range(1, NX)]

    def at_src(dl, dz, o=0):
        on = other if dl else line
        return (freqs[o], on * NZ + (z + dz + NZ) % NZ, rcv)

    def at_rcv(dh, dc, o=0):
        hy = 1 - high_y if dh else high_y
        return (freqs[o], src, hy * 2 + (1 - core if dc else core))

    near = [(0, 0), (1, 0), (0, 1), (0, -1), (0, 2), (0, -2)]
    peers = [at_src(*k, o) for k in near for o in range(NX) if k != (0, 0) or o]
    peers += [at_src(1, d) for d in (1, -1, 2, -2)]
    peers += [at_rcv(1, 0, o) for o in range(NX)] + [at_rcv(0, 1)]
    barrier = pltpu.get_barrier_semaphore()
    for peer in peers:
        pl.semaphore_signal(barrier, inc=1, device_id=peer, device_id_type=MESH)

    names = {}

    def copy(name, source, target, device):
        n = names.setdefault(name, len(names))
        return pltpu.make_async_remote_copy(
            src_ref=source, dst_ref=target, send_sem=send_sem.at[n], recv_sem=recv_sem.at[n],
            device_id=device, device_id_type=MESH,
        )

    def rows_at(dl, dz, part=None):
        block = (other if dl else line) * NZ + (z + dz + NZ) % NZ
        if part is None:
            return pl.ds(pl.multiple_of(block * ST, ST), ST)
        return pl.ds(pl.multiple_of(block * ST + part * (ST // 2), ST // 2), ST // 2)

    def rcv_rows(dh, dc):
        block = (1 - high_y if dh else high_y) * 2 + (1 - core if dc else core)
        return pl.ds(pl.multiple_of(block * ST, ST), ST)

    def prepare(j, _):
        block = reorder(refl[:, j].reshape(2 * SRC, RCV), 2 * NR, ST)
        block = reorder(block.T, NS, ST)
        high, low = halves(block)
        t_high[j] = high
        t_low[j] = low
        high, low = halves(block.T)
        r_high[j] = high
        r_low[j] = low
        return 0

    lax.fori_loop(0, BL, prepare, 0)
    whole = (ST * SH, FP, FP)
    eye = lax.broadcasted_iota(jnp.int32, whole, 1) == lax.broadcasted_iota(jnp.int32, whole, 2)
    for k, on in ((0, on_plus), (1, on_minus)):
        v = jnp.broadcast_to(on[...].astype(jnp.float32)[:, None, :], whole)
        v = jnp.sum(jnp.where(eye, v, 0.0), axis=2, keepdims=True)
        onset[k] = jnp.broadcast_to(v, (ST * SH, FP, LN))

    def load(ref, grp, i, lanes):
        parts = [
            ref[pl.ds(pl.multiple_of(s * ST + i * STEP, STEP), STEP), grp * PG : (grp + 1) * PG]
            for s in range(SH)
        ]
        x = parts[0] if SH == 1 else jnp.concatenate(parts, axis=1)
        return x.reshape(ROWS, lanes)

    def store(ref, grp, i, x):
        x = x.reshape(STEP, FP, NT)
        for s in range(SH):
            at = pl.ds(pl.multiple_of(s * ST + i * STEP, STEP), STEP)
            ref[at, grp * PG : (grp + 1) * PG] = x[:, s * PG : (s + 1) * PG]

    def keep(k, grp, i):
        t = lax.broadcasted_iota(jnp.int32, (ROWS, NT), 1).astype(jnp.float32)
        return t < load(onset.at[k], grp, i, LN)[:, 0:1]

    parts_of = ST // 8

    def pack_spec(grp):
        last = spec[grp, :, 4 * LN :]
        parts = [last[8 * b : 8 * b + 8] for b in range(parts_of)]
        for q in range(NX):
            piece[grp, q, 0:ST] = spec[grp, :, q * LN : (q + 1) * LN]
            piece[grp, q, ST : ST + 8] = pick(parts, q)

    def pack_bins(grp, n, blocks):
        parts = [blocks[4][8 * b : 8 * b + 8] for b in range(parts_of)]
        for q in range(NX):
            piece_sum[grp, n, q, 0:ST] = pick(blocks[:4], q)
            piece_sum[grp, n, q, ST : ST + 8] = pick(parts, q)

    def take_spec(grp, pieces):
        for q in range(NX):
            spec[grp, :, q * LN : (q + 1) * LN] = pieces[q][0:ST]
        parts = [pieces[q][ST : ST + 8] for q in range(NX)]
        for b in range(parts_of):
            spec[grp, 8 * b : 8 * b + 8, 4 * LN :] = pick(parts, b)

    def take_bins(pieces):
        full = [p[0:ST] for p in pieces]
        parts = [p[ST : ST + 8] for p in pieces]
        out = [pick(full, j) for j in range(4)]
        out.append(jnp.concatenate([pick(parts, b) for b in range(parts_of)], axis=0))
        return out

    def program(grp):
        def go(name, source, target, device):
            c = copy((grp,) + name, source, target, device)
            c.start()
            return c

        def spectrum_of(i, _):
            at = pl.ds(pl.multiple_of(i * STEP, STEP), STEP)
            spec[grp, at] = to_spectrum(load(direct, grp, i, NT), into, spread)
            return 0

        lax.fori_loop(0, ST // STEP, spectrum_of, 0)
        if grp == 0:
            pl.semaphore_wait(barrier, len(peers))

        for it in range(ITERS):
            pack_spec(grp)
            sent = []
            stage = {}
            for n in (4, 5, 2, 3, 1, 0):
                for o in (2, 1, 3, 0):
                    if n or o:
                        c = go(
                            ("g", n, o), piece.at[grp, freqs[o]], land_g.at[grp, n, f],
                            at_src(*near[n], o),
                        )
                        stage.setdefault(n, []).append(c)
                        sent.append(c)
            land_g[grp, 0, f] = piece[grp, f]
            late = []

            def arrive(n):
                for c in stage[n]:
                    c.wait_recv()
                dl, dz = near[n]
                at = rows_at(dl, -dz)
                blocks = take_bins([land_g[grp, n, q] for q in range(NX)])
                for j in range(BL):
                    xs[grp, j, at] = blocks[j]
                return at

            def forward_to(name, at, dl, dz):
                c = go(name, xs.at[grp, :, at], xs.at[grp, :, at], at_src(dl, dz))
                late.append(c)
                sent.append(c)

            yield
            for n in (2, 3):
                at = arrive(n)
                forward_to(("gy", n), at, 1, 0)
            yield
            for n, w, way in ((4, 0, 1), (5, 1, -1)):
                at = arrive(n)
                half = rows_at(0, -2 * way, w)
                forward_to(("gd", n), at, 1, way)
                forward_to(("g3", n), at, 0, way)
                forward_to(("ge", n), half, 1, 2 * way)
                forward_to(("g4", n), half, 0, 2 * way)
                forward_to(("gy", n), at, 1, 0)
            arrive(0)
            arrive(1)
            yield
            for c in late:
                c.wait_recv()
            for c in sent:
                c.wait_send()

            def forward(j, _):
                x_high, x_low = halves(unfold(xs[grp, j]))
                both = mm(r_high[j], jnp.concatenate([x_high, x_low], axis=1))
                g = fold(both[:, :LN] + both[:, LN:] + mm(r_low[j], x_high))
                n = SRC // SH
                real = is_real((n, LN))
                turned = swap_parts(g[n:], real)
                y[grp, j] = g[:n] + jnp.where(real, -turned, turned)
                return 0

            lax.fori_loop(0, BL, forward, 0)

            pair = [
                go(("ra", dh), y.at[grp, :, rcv_rows(dh, 1)], r4a.at[grp, dh], at_rcv(0, 1))
                for dh in (1, 0)
            ]
            yield
            sent = list(pair)
            stage = []
            for dh, c in zip((1, 0), pair):
                c.wait_recv()
                total = y[grp, :, rcv_rows(dh, 0)] + r4a[grp, dh]
                pack_bins(grp, dh, [total[j] for j in range(BL)])
                for o in (2, 1, 3, 0):
                    if dh or o:
                        stage.append(
                            go(
                                ("rx", dh, o), piece_sum.at[grp, dh, freqs[o]],
                                land_r.at[grp, dh, f], at_rcv(dh, 0, o),
                            )
                        )
            land_r[grp, 0, f] = piece_sum[grp, 0, f]
            yield
            for c in stage:
                c.wait_recv()
            for c in sent + stage:
                c.wait_send()
            take_spec(grp, [land_r[grp, 0, q] + land_r[grp, 1, q] for q in range(NX)])

            def up(i, _):
                at = pl.ds(pl.multiple_of(i * STEP, STEP), STEP)
                x = jnp.where(keep(1, grp, i), to_time(spec[grp, at], collect, back), 0.0)
                store(out_minus, grp, i, x)
                spec[grp, at] = to_spectrum(x, into, spread)
                return 0

            lax.fori_loop(0, ST // STEP, up, 0)

            pack_spec(grp)
            stage = [[], []]
            for dh in (1, 0):
                for o in (2, 1, 3, 0):
                    if dh or o:
                        stage[dh].append(
                            go(
                                ("cx", dh, o), piece.at[grp, freqs[o]], land_f.at[grp, dh, f],
                                at_rcv(dh, 0, o),
                            )
                        )
            land_f[grp, 0, f] = piece[grp, f]
            yield
            pair = []
            for dh in (0, 1):
                for c in stage[dh]:
                    c.wait_recv()
                at = rcv_rows(dh, 0)
                blocks = take_bins([land_f[grp, dh, q] for q in range(NX)])
                for j in range(BL):
                    cs[grp, j, at] = blocks[j]
                pair.append(go(("cc", dh), cs.at[grp, :, at], cs.at[grp, :, at], at_rcv(0, 1)))
            yield
            for c in pair:
                c.wait_recv()
            for c in pair + stage[0] + stage[1]:
                c.wait_send()

            def adjoint(j, _):
                block = cs[grp, j]
                real = is_real(block.shape)
                turned = swap_parts(block, real)
                both = jnp.concatenate([block, jnp.where(real, turned, -turned)], axis=0)
                c_high, c_low = halves(unfold(both))
                both = mm(t_high[j], jnp.concatenate([c_high, c_low], axis=1))
                h[grp, j] = fold(both[:, :LN] + both[:, LN:] + mm(t_low[j], c_high))
                return 0

            lax.fori_loop(0, BL, adjoint, 0)

            sent = []
            stage = {}

            def part_to(name, slot, dl, dist, dest, part=None):
                target = rs.at[grp, slot]
                if part is not None:
                    target = rs.at[grp, slot, :, pl.ds(part * (ST // 2), ST // 2)]
                c = go(name, h.at[grp, :, rows_at(dl, dist, part)], target, at_src(*dest))
                stage[slot] = stage.get(slot, []) + [c]
                sent.append(c)

            for w, way in ((0, 1), (1, -1)):
                part_to(("se", w), 8 + w, 1, 4, (1, 2 * way), w)
                part_to(("s4", w), 6 + w, 0, 4, (0, 2 * way), w)
                part_to(("sd", w), 4 + w, 1, 3 * way, (1, way))
                part_to(("s3", w), 2 + w, 0, 3 * way, (0, way))
            for w, way in ((0, 1), (1, -1)):
                part_to(("sy", 2, w), 10 + w, 1, 2 * way, (1, 0))
            for w, way in ((0, 1), (1, -1)):
                part_to(("sy", 1, w), w, 1, way, (1, 0))

            last = {}

            def finish(n, blocks):
                pack_bins(grp, n, blocks)
                for o in (2, 1, 3, 0):
                    if n or o:
                        c = go(
                            ("sx", n, o), piece_sum.at[grp, n, freqs[o]], land_s.at[grp, n, f],
                            at_src(*near[n], o),
                        )
                        last.setdefault(n, []).append(c)
                        sent.append(c)

            def bins_of(total):
                return [total[j] for j in range(BL)]

            finish(1, [h[grp, j, rows_at(1, 0)] for j in range(BL)])
            finish(0, [h[grp, j, rows_at(0, 0)] for j in range(BL)])
            land_s[grp, 0, f] = piece_sum[grp, 0, f]
            yield
            for w, way in ((0, 1), (1, -1)):
                for c in stage[w]:
                    c.wait_recv()
                finish(2 + w, bins_of(h[grp, :, rows_at(0, way)] + rs[grp, w]))
            yield
            for w, way in ((0, 1), (1, -1)):
                for slot in (2 + w, 4 + w, 6 + w, 8 + w, 10 + w):
                    for c in stage[slot]:
                        c.wait_recv()
                total = h[grp, :, rows_at(0, 2 * way)] + rs[grp, 2 + w] + rs[grp, 4 + w]
                total = total + rs[grp, 10 + w]
                half = slice(w * (ST // 2), (w + 1) * (ST // 2))
                four = rs[grp, 6 + w, :, half] + rs[grp, 8 + w, :, half]
                some = [total[:, :8], total[:, 8:]] if ST == 16 else [total[:, :16], total[:, 16:]]
                some[w] = some[w] + four
                finish(4 + w, bins_of(jnp.concatenate(some, axis=1)))
            yield
            for n in range(6):
                for c in last[n]:
                    c.wait_recv()
            for c in sent:
                c.wait_send()
            pieces = []
            for q in range(NX):
                total = land_s[grp, 0, q]
                for n in range(1, 6):
                    total = total + land_s[grp, n, q]
                pieces.append(total)
            take_spec(grp, pieces)

            def down(i, _):
                at = pl.ds(pl.multiple_of(i * STEP, STEP), STEP)
                x = jnp.where(keep(0, grp, i), to_time(spec[grp, at], collect, back), 0.0)
                x = load(direct, grp, i, NT) + x
                if it < ITERS - 1:
                    spec[grp, at] = to_spectrum(x, into, spread)
                else:
                    store(out_plus, grp, i, x)
                return 0

            lax.fori_loop(0, ST // STEP, down, 0)

    running = [program(grp) for grp in range(GROUPS)]
    while running:
        for p in list(running):
            if next(p, 0) == 0:
                running.remove(p)


MESSAGES = 88 * GROUPS


def per_device(direct, reflection, onset_plus, onset_minus):
    vmem = pl.BlockSpec(memory_space=pltpu.VMEM)
    f32, bf16 = jnp.float32, jnp.bfloat16
    traces = jax.ShapeDtypeStruct((ST * SH, FP, NT), f32)
    return pl.pallas_call(
        kernel,
        out_shape=(traces, traces),
        in_specs=[vmem] * 8,
        out_specs=(vmem, vmem),
        scratch_shapes=[
            pltpu.VMEM((BL, 2 * SRC, RCV), bf16),
            pltpu.VMEM((BL, 2 * SRC, RCV), bf16),
            pltpu.VMEM((BL, RCV, 2 * SRC), bf16),
            pltpu.VMEM((BL, RCV, 2 * SRC), bf16),
            pltpu.VMEM((2, ST * SH, FP, LN), f32),
            pltpu.VMEM((GROUPS, ST, WIDE), f32),
            pltpu.VMEM((GROUPS, NX, PR, LN), f32),
            pltpu.VMEM((GROUPS, 6, NX, PR, LN), f32),
            pltpu.VMEM((GROUPS, 6, NX, PR, LN), f32),
            pltpu.VMEM((GROUPS, 2, NX, PR, LN), f32),
            pltpu.VMEM((GROUPS, 2, NX, PR, LN), f32),
            pltpu.VMEM((GROUPS, 6, NX, PR, LN), f32),
            pltpu.VMEM((GROUPS, BL, NS * ST, LN), f32),
            pltpu.VMEM((GROUPS, BL, NR * ST, LN), f32),
            pltpu.VMEM((GROUPS, 2, BL, ST, LN), f32),
            pltpu.VMEM((GROUPS, BL, NR * ST, LN), f32),
            pltpu.VMEM((GROUPS, BL, NS * ST, LN), f32),
            pltpu.VMEM((GROUPS, 12, BL, ST, LN), f32),
            pltpu.SemaphoreType.DMA((MESSAGES,)),
            pltpu.SemaphoreType.DMA((MESSAGES,)),
        ],
        compiler_params=pltpu.CompilerParams(
            collective_id=0, has_side_effects=True, vmem_limit_bytes=56 * 1024 * 1024
        ),
    )(direct, reflection, onset_plus, onset_minus, *[jnp.asarray(a) for a in tables()])


def solution(mesh):
    in_specs = (
        P(("rcv", "src"), "freq", None),
        P(None, "freq", "src", "rcv"),
        P(("rcv", "src"), "freq"),
        P(("src", "rcv"), "freq"),
    )
    out_specs = (P(("rcv", "src"), "freq", None), P(("src", "rcv"), "freq", None))
    return jax.shard_map(
        per_device, mesh=mesh, in_specs=in_specs, out_specs=out_specs, check_vma=False
    )
```

time: 668 us -> 153 us (0.23)
  waiting for transfers between devices: 413 us -> 0 us
  Pallas kernels: 0 us -> 143 us
  blocking collectives: 107 us -> 0 us
  matrix products: 74.6 us -> 0 us
  local copies, waits for them, and re-layouts: 34.7 us -> 7.38 us
  between operations: 15.2 us -> 0.65 us
  starting transfers between devices: 9.51 us -> 0 us
  other arithmetic: 7.39 us -> 0 us
    reduce_scatter x4 -> x0, waiting for transfers between devices: 203 us -> none  [the longest x2 148 us: per_device(): lax.psum_scatter(combine_adjoint(first_part, second_part, half_width), 's...]
    all_gather x2 -> x0, waiting for transfers between devices: 199 us -> none  [per_device(): gathered = lax.all_gather(spectrum, 'src', axis=0, tiled=True)]
    pallas_call x0 -> x1, Pallas kernels: none -> 143 us  [per_device(): pl.pallas_call(kernel, out_shape=(traces, traces), in_specs=[vmem] * 8, o...]
    all_to_all x6 -> x0, blocking collectives: 91.4 us -> none  [the longest x2 55.4 us: per_device(): lax.all_to_all(gathered, 'freq', split_axis=1, concat_axis=3, tiled=True)]
    dot_general x24 -> x0, matrix products: 74.6 us -> none  [the longest x4 22.6 us: to_spectrum(): jnp.einsum('spt,tj->sjp', traces, sine_table, precision=HIGHEST)]
    all_gather x2 -> x0, blocking collectives: 15.3 us -> none  [per_device(): source_spec = lax.all_gather(regrouped, 'rcv', axis=0, tiled=True)]
    all_gather x2 -> x0, local copies, waits for them, and re-layouts: 12.7 us -> none  [per_device(): gathered = lax.all_gather(spectrum, 'src', axis=0, tiled=True)]
    all_to_all x2 -> x0, waiting for transfers between devices: 10.8 us -> none  [the longest x1 5.63 us: per_device(): lax.all_to_all(summed, 'freq', split_axis=3, concat_axis=1, tiled=True)]
  transfers between devices with their start and end apart: 8 -> 0, of which waited for: 8 -> 0; matrix products, arithmetic and copies ran while one was open for 0% -> 0% of each run, Pallas kernels for 0% -> 0%
where the time goes in v2:
time: 153 us; the launch traced here: 152 us
  Pallas kernels  143 us (93%)
  local copies, waits for them, and re-layouts  7.38 us (5%)
    pallas_call x1, Pallas kernels, per_device(): pl.pallas_call(kernel, out_shape=(traces, traces), in_specs=[vmem] * 8, o...  143 us
    unnamed x6, local copies, waits for them, and re-layouts  7.38 us

profile of v2, /device:TPU:16, one launch (start us, length us, event | category | flops | bytes accessed | tf_op | source)
XLA Modules:
  0.0 151.5 jit_solution(8500013517390585099)
XLA Ops:
  0.6 1.4 copy.10.on_plus
  2.0 1.4 copy.11.on_minus
  3.4 143.5 %shard_map.95 = (f32[32,16,1024]{2,1,0:T(8,128)}, f32[32,16,1024]{2,1,0:T(8,128)}) custom-call(f32[32,16,1024]{2,1,0:T(8,128)} %direct.1, f32[2,5,128,512]{3,2,1,0:T(8,128)} %refl.1, s32[32,16]{1,0:T(8,128)} %copy.10.on_plus, s32[32,16]{1,0:T(8,128)} %copy.11.on_minus, bf16[2,1024,128]{2,1,0:T(8,128)(2,1)} %constant.8.clone.into, ...), custom_call_target="tpu_custom_call" | custom-call | tf_op jit(solution)/shard_map/pallas_call | solution.py:526
  146.9 0.0 copy-start
  146.9 3.3 %copy.14 = f32[32,16,1024]{2,1,0:T(8,128)} copy(f32[32,16,1024]{2,1,0:T(8,128)} %get-tuple-element.4) | data formatting | bytes 4194304
  150.2 0.0 copy-done
  150.2 1.3 copy.15
Async XLA Ops:
  146.9 3.3 %copy-start = (f32[32,16,1024]{2,1,0:T(8,128)S(1)}, f32[32,16,1024]{2,1,0:T(8,128)}, u32[]{:S(2)}) copy-start(f32[32,16,1024]{2,1,0:T(8,128)} %get-tuple-element.5) | copy-start | bytes 6291460

commit v3 on v2

--- a/solution.py
+++ b/solution.py
@@ -220,7 +220,7 @@
     whole = (ST * SH, FP, FP)
     eye = lax.broadcasted_iota(jnp.int32, whole, 1) == lax.broadcasted_iota(jnp.int32, whole, 2)
     for k, on in ((0, on_plus), (1, on_minus)):
-        v = jnp.broadcast_to(on[...].astype(jnp.float32)[:, None, :], whole)
+        v = jnp.broadcast_to(on[...].astype(jnp.float32).T[:, None, :], whole)
         v = jnp.sum(jnp.where(eye, v, 0.0), axis=2, keepdims=True)
         onset[k] = jnp.broadcast_to(v, (ST * SH, FP, LN))
 
@@ -282,7 +282,7 @@
             spec[grp, at] = to_spectrum(load(direct, grp, i, NT), into, spread)
             return 0
 
-        lax.fori_loop(0, ST // STEP, spectrum_of, 0)
+        lax.fori_loop(0, ST // STEP, spectrum_of, 0, unroll=True)
         if grp == 0:
             pl.semaphore_wait(barrier, len(peers))
 
@@ -348,7 +348,7 @@
                 y[grp, j] = g[:n] + jnp.where(real, -turned, turned)
                 return 0
 
-            lax.fori_loop(0, BL, forward, 0)
+            lax.fori_loop(0, BL, forward, 0, unroll=True)
 
             pair = [
                 go(("ra", dh), y.at[grp, :, rcv_rows(dh, 1)], r4a.at[grp, dh], at_rcv(0, 1))
@@ -384,7 +384,7 @@
                 spec[grp, at] = to_spectrum(x, into, spread)
                 return 0
 
-            lax.fori_loop(0, ST // STEP, up, 0)
+            lax.fori_loop(0, ST // STEP, up, 0, unroll=True)
 
             pack_spec(grp)
             stage = [[], []]
@@ -424,7 +424,7 @@
                 h[grp, j] = fold(both[:, :LN] + both[:, LN:] + mm(t_low[j], c_high))
                 return 0
 
-            lax.fori_loop(0, BL, adjoint, 0)
+            lax.fori_loop(0, BL, adjoint, 0, unroll=True)
 
             sent = []
             stage = {}
@@ -507,7 +507,7 @@
                     store(out_plus, grp, i, x)
                 return 0
 
-            lax.fori_loop(0, ST // STEP, down, 0)
+            lax.fori_loop(0, ST // STEP, down, 0, unroll=True)
 
     running = [program(grp) for grp in range(GROUPS)]
     while running:
@@ -553,7 +553,7 @@
         compiler_params=pltpu.CompilerParams(
             collective_id=0, has_side_effects=True, vmem_limit_bytes=56 * 1024 * 1024
         ),
-    )(direct, reflection, onset_plus, onset_minus, *[jnp.asarray(a) for a in tables()])
+    )(direct, reflection, onset_plus.T, onset_minus.T, *[jnp.asarray(a) for a in tables()])
 
 
 def solution(mesh):

time: 153 us -> 140 us (0.915)
  Pallas kernels: 143 us -> 133 us
  local copies, waits for them, and re-layouts: 7.38 us -> 4.63 us
    pallas_call x1, Pallas kernels: 143 us -> 133 us  [per_device(): pl.pallas_call(kernel, out_shape=(traces, traces), in_specs=[vmem] * 8, o...]
    unnamed x6 -> x4, local copies, waits for them, and re-layouts: 7.38 us -> 4.63 us
where the time goes in v3:
time: 140 us; the launch traced here: 138 us
  Pallas kernels  133 us (95%)
  local copies, waits for them, and re-layouts  4.63 us (3%)
    pallas_call x1, Pallas kernels, per_device(): pl.pallas_call(kernel, out_shape=(traces, traces), in_specs=[vmem] * 8, o...  133 us
    unnamed x4, local copies, waits for them, and re-layouts  4.63 us

profile of v3, /device:TPU:16, one launch (start us, length us, event | category | flops | bytes accessed | tf_op | source)
XLA Modules:
  0.0 138.1 jit_solution(13421873847302511353)
XLA Ops:
  0.6 132.8 %shard_map.95 = (f32[32,16,1024]{2,1,0:T(8,128)}, f32[32,16,1024]{2,1,0:T(8,128)}) custom-call(f32[32,16,1024]{2,1,0:T(8,128)} %direct.1, f32[2,5,128,512]{3,2,1,0:T(8,128)} %refl.1, s32[16,32]{1,0:T(8,128)} %bitcast.2, s32[16,32]{1,0:T(8,128)} %bitcast.3, bf16[2,1024,128]{2,1,0:T(8,128)(2,1)} %constant.8.clone.into, bf16[128,640]{1,0:T(8,128)(2,1)} %constant.9.clone.spread, ...), custom_call_target="tpu_custom_call" | custom-call | tf_op jit(solution)/shard_map/pallas_call | solution.py:526
  133.4 0.0 copy-start
  133.5 3.3 %copy.12 = f32[32,16,1024]{2,1,0:T(8,128)} copy(f32[32,16,1024]{2,1,0:T(8,128)} %get-tuple-element.4) | data formatting | bytes 4194304
  136.8 0.0 copy-done
  136.8 1.3 copy.13
Async XLA Ops:
  133.4 3.3 %copy-start = (f32[32,16,1024]{2,1,0:T(8,128)S(1)}, f32[32,16,1024]{2,1,0:T(8,128)}, u32[]{:S(2)}) copy-start(f32[32,16,1024]{2,1,0:T(8,128)} %get-tuple-element.5) | copy-start | bytes 6291460

commit v4 on v3

--- a/solution.py
+++ b/solution.py
@@ -26,8 +26,9 @@
 LN = 128
 SRC = 128
 RCV = 512
-NS = 16
+HALF = RCV // 2
 NR = 4
+NY = 2 * NR
 PR = ST + 8
 COLS = 2 * NF
 WIDE = COLS * FP
@@ -157,7 +158,7 @@
 def kernel(
     direct, refl, on_plus, on_minus, into, spread, collect, back,
     out_plus, out_minus,
-    r_high, r_low, t_high, t_low, onset, spec, piece, piece_sum, land_g, land_r, land_f, land_s,
+    r_land, r_high, r_low, t_high, t_low, onset, spec, piece, piece_sum, land_g, land_r, land_f, land_s,
     xs, y, r4a, cs, h, rs, send_sem, recv_sem,
 ):
     f = lax.axis_index("freq")
@@ -174,14 +175,15 @@
         on = other if dl else line
         return (freqs[o], on * NZ + (z + dz + NZ) % NZ, rcv)
 
-    def at_rcv(dh, dc, o=0):
+    def at_rcv(dl, dh, dc, o=0):
         hy = 1 - high_y if dh else high_y
-        return (freqs[o], src, hy * 2 + (1 - core if dc else core))
-
-    near = [(0, 0), (1, 0), (0, 1), (0, -1), (0, 2), (0, -2)]
-    peers = [at_src(*k, o) for k in near for o in range(NX) if k != (0, 0) or o]
-    peers += [at_src(1, d) for d in (1, -1, 2, -2)]
-    peers += [at_rcv(1, 0, o) for o in range(NX)] + [at_rcv(0, 1)]
+        on = other if dl else line
+        return (freqs[o], on * NZ + z, hy * 2 + (1 - core if dc else core))
+
+    near = [0, 1, -1, 2, -2]
+    column = [(0, 0), (1, 0), (0, 1), (1, 1)]
+    peers = [at_src(0, k, o) for k in near for o in range(NX) if k or o]
+    peers += [at_rcv(*k, 0, o) for k in column[1:] for o in range(NX)] + [at_rcv(0, 0, 1)]
     barrier = pltpu.get_barrier_semaphore()
     for peer in peers:
         pl.semaphore_signal(barrier, inc=1, device_id=peer, device_id_type=MESH)
@@ -195,34 +197,51 @@
             device_id=device, device_id_type=MESH,
         )
 
-    def rows_at(dl, dz, part=None):
-        block = (other if dl else line) * NZ + (z + dz + NZ) % NZ
+    def rows_at(dz, part=None):
+        block = (z + dz + NZ) % NZ
         if part is None:
             return pl.ds(pl.multiple_of(block * ST, ST), ST)
         return pl.ds(pl.multiple_of(block * ST + part * (ST // 2), ST // 2), ST // 2)
 
-    def rcv_rows(dh, dc):
+    def rcv_rows(dl, dh, dc):
         block = (1 - high_y if dh else high_y) * 2 + (1 - core if dc else core)
-        return pl.ds(pl.multiple_of(block * ST, ST), ST)
-
-    def prepare(j, _):
-        block = reorder(refl[:, j].reshape(2 * SRC, RCV), 2 * NR, ST)
-        block = reorder(block.T, NS, ST)
+        return pl.ds(pl.multiple_of((dl * NR + block) * ST, ST), ST)
+
+    def lanes_of(on):
+        return pl.ds(pl.multiple_of(on * HALF, HALF), HALF)
+
+    swap = [
+        copy(("r", j), refl.at[:, j, :, lanes_of(other)], r_land.at[j], at_rcv(1, 0, 0))
+        for j in range(BL)
+    ]
+
+    def prepare(j):
+        both = (refl[:, j, :, lanes_of(line)], r_land[j])
+        block = jnp.concatenate(
+            [
+                b[c, (k * SH + s) * ST : (k * SH + s + 1) * ST]
+                for s in range(SH)
+                for c in range(2)
+                for b in both
+                for k in range(NR)
+            ],
+            axis=0,
+        )
+        block = reorder(block.T, NZ, ST)
         high, low = halves(block)
         t_high[j] = high
         t_low[j] = low
         high, low = halves(block.T)
         r_high[j] = high
         r_low[j] = low
-        return 0
-
-    lax.fori_loop(0, BL, prepare, 0)
-    whole = (ST * SH, FP, FP)
-    eye = lax.broadcasted_iota(jnp.int32, whole, 1) == lax.broadcasted_iota(jnp.int32, whole, 2)
-    for k, on in ((0, on_plus), (1, on_minus)):
-        v = jnp.broadcast_to(on[...].astype(jnp.float32).T[:, None, :], whole)
-        v = jnp.sum(jnp.where(eye, v, 0.0), axis=2, keepdims=True)
-        onset[k] = jnp.broadcast_to(v, (ST * SH, FP, LN))
+
+    def prepare_onsets():
+        whole = (ST * SH, FP, FP)
+        eye = lax.broadcasted_iota(jnp.int32, whole, 1) == lax.broadcasted_iota(jnp.int32, whole, 2)
+        for k, on in ((0, on_plus), (1, on_minus)):
+            v = jnp.broadcast_to(on[...].astype(jnp.float32).T[:, None, :], whole)
+            v = jnp.sum(jnp.where(eye, v, 0.0), axis=2, keepdims=True)
+            onset[k] = jnp.broadcast_to(v, (ST * SH, FP, LN))
 
     def load(ref, grp, i, lanes):
         parts = [
@@ -285,17 +304,19 @@
         lax.fori_loop(0, ST // STEP, spectrum_of, 0, unroll=True)
         if grp == 0:
             pl.semaphore_wait(barrier, len(peers))
+            for c in swap:
+                c.start()
 
         for it in range(ITERS):
             pack_spec(grp)
             sent = []
             stage = {}
-            for n in (4, 5, 2, 3, 1, 0):
+            for n in (3, 4, 1, 2, 0):
                 for o in (2, 1, 3, 0):
                     if n or o:
                         c = go(
                             ("g", n, o), piece.at[grp, freqs[o]], land_g.at[grp, n, f],
-                            at_src(*near[n], o),
+                            at_src(0, near[n], o),
                         )
                         stage.setdefault(n, []).append(c)
                         sent.append(c)
@@ -305,33 +326,26 @@
             def arrive(n):
                 for c in stage[n]:
                     c.wait_recv()
-                dl, dz = near[n]
-                at = rows_at(dl, -dz)
+                at = rows_at(-near[n])
                 blocks = take_bins([land_g[grp, n, q] for q in range(NX)])
                 for j in range(BL):
                     xs[grp, j, at] = blocks[j]
                 return at
 
-            def forward_to(name, at, dl, dz):
-                c = go(name, xs.at[grp, :, at], xs.at[grp, :, at], at_src(dl, dz))
+            def forward_to(name, at, dz):
+                c = go(name, xs.at[grp, :, at], xs.at[grp, :, at], at_src(0, dz))
                 late.append(c)
                 sent.append(c)
 
-            yield
-            for n in (2, 3):
+            if it == 0 and grp == GROUPS - 1:
+                prepare_onsets()
+            yield
+            for n, w, way in ((3, 0, 1), (4, 1, -1)):
                 at = arrive(n)
-                forward_to(("gy", n), at, 1, 0)
-            yield
-            for n, w, way in ((4, 0, 1), (5, 1, -1)):
-                at = arrive(n)
-                half = rows_at(0, -2 * way, w)
-                forward_to(("gd", n), at, 1, way)
-                forward_to(("g3", n), at, 0, way)
-                forward_to(("ge", n), half, 1, 2 * way)
-                forward_to(("g4", n), half, 0, 2 * way)
-                forward_to(("gy", n), at, 1, 0)
-            arrive(0)
-            arrive(1)
+                forward_to(("g3", n), at, way)
+                forward_to(("g4", n), rows_at(-2 * way, w), 2 * way)
+            for n in (1, 2, 0):
+                arrive(n)
             yield
             for c in late:
                 c.wait_recv()
@@ -342,40 +356,53 @@
                 x_high, x_low = halves(unfold(xs[grp, j]))
                 both = mm(r_high[j], jnp.concatenate([x_high, x_low], axis=1))
                 g = fold(both[:, :LN] + both[:, LN:] + mm(r_low[j], x_high))
-                n = SRC // SH
+                n = 2 * SRC // SH
                 real = is_real((n, LN))
                 turned = swap_parts(g[n:], real)
                 y[grp, j] = g[:n] + jnp.where(real, -turned, turned)
                 return 0
 
-            lax.fori_loop(0, BL, forward, 0, unroll=True)
-
-            pair = [
-                go(("ra", dh), y.at[grp, :, rcv_rows(dh, 1)], r4a.at[grp, dh], at_rcv(0, 1))
-                for dh in (1, 0)
-            ]
-            yield
-            sent = list(pair)
+            for j in range(BL):
+                if it == 0 and grp == 0:
+                    swap[j].wait_recv()
+                    prepare(j)
+                forward(j, 0)
+
+            order = (2, 3, 1, 0)
+            pair = {
+                n: go(
+                    ("ra", n), y.at[grp, :, rcv_rows(*column[n], 1)], r4a.at[grp, n],
+                    at_rcv(0, 0, 1),
+                )
+                for n in order
+            }
+            yield
             stage = []
-            for dh, c in zip((1, 0), pair):
-                c.wait_recv()
-                total = y[grp, :, rcv_rows(dh, 0)] + r4a[grp, dh]
-                pack_bins(grp, dh, [total[j] for j in range(BL)])
+            for n in order:
+                pair[n].wait_recv()
+                total = y[grp, :, rcv_rows(*column[n], 0)] + r4a[grp, n]
+                pack_bins(grp, n, [total[j] for j in range(BL)])
                 for o in (2, 1, 3, 0):
-                    if dh or o:
+                    if n or o:
                         stage.append(
                             go(
-                                ("rx", dh, o), piece_sum.at[grp, dh, freqs[o]],
-                                land_r.at[grp, dh, f], at_rcv(dh, 0, o),
+                                ("rx", n, o), piece_sum.at[grp, n, freqs[o]],
+                                land_r.at[grp, n, f], at_rcv(*column[n], 0, o),
                             )
                         )
             land_r[grp, 0, f] = piece_sum[grp, 0, f]
             yield
             for c in stage:
                 c.wait_recv()
-            for c in sent + stage:
+            for c in list(pair.values()) + stage:
                 c.wait_send()
-            take_spec(grp, [land_r[grp, 0, q] + land_r[grp, 1, q] for q in range(NX)])
+            take_spec(
+                grp,
+                [
+                    (land_r[grp, 0, q] + land_r[grp, 1, q]) + (land_r[grp, 2, q] + land_r[grp, 3, q])
+                    for q in range(NX)
+                ],
+            )
 
             def up(i, _):
                 at = pl.ds(pl.multiple_of(i * STEP, STEP), STEP)
@@ -387,31 +414,32 @@
             lax.fori_loop(0, ST // STEP, up, 0, unroll=True)
 
             pack_spec(grp)
-            stage = [[], []]
-            for dh in (1, 0):
+            stage = {}
+            for n in order:
                 for o in (2, 1, 3, 0):
-                    if dh or o:
-                        stage[dh].append(
-                            go(
-                                ("cx", dh, o), piece.at[grp, freqs[o]], land_f.at[grp, dh, f],
-                                at_rcv(dh, 0, o),
-                            )
+                    if n or o:
+                        c = go(
+                            ("cx", n, o), piece.at[grp, freqs[o]], land_f.at[grp, n, f],
+                            at_rcv(*column[n], 0, o),
                         )
+                        stage.setdefault(n, []).append(c)
             land_f[grp, 0, f] = piece[grp, f]
             yield
             pair = []
-            for dh in (0, 1):
-                for c in stage[dh]:
+            for n in (0, 1, 3, 2):
+                for c in stage[n]:
                     c.wait_recv()
-                at = rcv_rows(dh, 0)
-                blocks = take_bins([land_f[grp, dh, q] for q in range(NX)])
+                at = rcv_rows(*column[n], 0)
+                blocks = take_bins([land_f[grp, n, q] for q in range(NX)])
                 for j in range(BL):
                     cs[grp, j, at] = blocks[j]
-                pair.append(go(("cc", dh), cs.at[grp, :, at], cs.at[grp, :, at], at_rcv(0, 1)))
+                pair.append(
+                    go(("cc", n), cs.at[grp, :, at], cs.at[grp, :, at], at_rcv(0, 0, 1))
+                )
             yield
             for c in pair:
                 c.wait_recv()
-            for c in pair + stage[0] + stage[1]:
+            for c in pair + [c for n in order for c in stage[n]]:
                 c.wait_send()
 
             def adjoint(j, _):
@@ -424,28 +452,23 @@
                 h[grp, j] = fold(both[:, :LN] + both[:, LN:] + mm(t_low[j], c_high))
                 return 0
 
-            lax.fori_loop(0, BL, adjoint, 0, unroll=True)
+            for j in range(BL):
+                adjoint(j, 0)
 
             sent = []
-            stage = {}
-
-            def part_to(name, slot, dl, dist, dest, part=None):
+            stage = [[], []]
+
+            def part_to(name, w, slot, dist, dz, part=None):
                 target = rs.at[grp, slot]
                 if part is not None:
                     target = rs.at[grp, slot, :, pl.ds(part * (ST // 2), ST // 2)]
-                c = go(name, h.at[grp, :, rows_at(dl, dist, part)], target, at_src(*dest))
-                stage[slot] = stage.get(slot, []) + [c]
+                c = go(name, h.at[grp, :, rows_at(dist, part)], target, at_src(0, dz))
+                stage[w].append(c)
                 sent.append(c)
 
             for w, way in ((0, 1), (1, -1)):
-                part_to(("se", w), 8 + w, 1, 4, (1, 2 * way), w)
-                part_to(("s4", w), 6 + w, 0, 4, (0, 2 * way), w)
-                part_to(("sd", w), 4 + w, 1, 3 * way, (1, way))
-                part_to(("s3", w), 2 + w, 0, 3 * way, (0, way))
-            for w, way in ((0, 1), (1, -1)):
-                part_to(("sy", 2, w), 10 + w, 1, 2 * way, (1, 0))
-            for w, way in ((0, 1), (1, -1)):
-                part_to(("sy", 1, w), w, 1, way, (1, 0))
+                part_to(("s4", w), w, 2 + w, 4, 2 * way, w)
+                part_to(("s3", w), w, w, 3 * way, way)
 
             last = {}
 
@@ -455,7 +478,7 @@
                     if n or o:
                         c = go(
                             ("sx", n, o), piece_sum.at[grp, n, freqs[o]], land_s.at[grp, n, f],
-                            at_src(*near[n], o),
+                            at_src(0, near[n], o),
                         )
                         last.setdefault(n, []).append(c)
                         sent.append(c)
@@ -463,28 +486,21 @@
             def bins_of(total):
                 return [total[j] for j in range(BL)]
 
-            finish(1, [h[grp, j, rows_at(1, 0)] for j in range(BL)])
-            finish(0, [h[grp, j, rows_at(0, 0)] for j in range(BL)])
+            finish(1, [h[grp, j, rows_at(1)] for j in range(BL)])
+            finish(2, [h[grp, j, rows_at(-1)] for j in range(BL)])
+            finish(0, [h[grp, j, rows_at(0)] for j in range(BL)])
             land_s[grp, 0, f] = piece_sum[grp, 0, f]
             yield
             for w, way in ((0, 1), (1, -1)):
                 for c in stage[w]:
                     c.wait_recv()
-                finish(2 + w, bins_of(h[grp, :, rows_at(0, way)] + rs[grp, w]))
-            yield
-            for w, way in ((0, 1), (1, -1)):
-                for slot in (2 + w, 4 + w, 6 + w, 8 + w, 10 + w):
-                    for c in stage[slot]:
-                        c.wait_recv()
-                total = h[grp, :, rows_at(0, 2 * way)] + rs[grp, 2 + w] + rs[grp, 4 + w]
-                total = total + rs[grp, 10 + w]
+                total = h[grp, :, rows_at(2 * way)] + rs[grp, w]
                 half = slice(w * (ST // 2), (w + 1) * (ST // 2))
-                four = rs[grp, 6 + w, :, half] + rs[grp, 8 + w, :, half]
-                some = [total[:, :8], total[:, 8:]] if ST == 16 else [total[:, :16], total[:, 16:]]
-                some[w] = some[w] + four
-                finish(4 + w, bins_of(jnp.concatenate(some, axis=1)))
-            yield
-            for n in range(6):
+                some = [total[:, : ST // 2], total[:, ST // 2 :]]
+                some[w] = some[w] + rs[grp, 2 + w, :, half]
+                finish(3 + w, bins_of(jnp.concatenate(some, axis=1)))
+            yield
+            for n in range(5):
                 for c in last[n]:
                     c.wait_recv()
             for c in sent:
@@ -492,7 +508,7 @@
             pieces = []
             for q in range(NX):
                 total = land_s[grp, 0, q]
-                for n in range(1, 6):
+                for n in range(1, 5):
                     total = total + land_s[grp, n, q]
                 pieces.append(total)
             take_spec(grp, pieces)
@@ -514,9 +530,11 @@
         for p in list(running):
             if next(p, 0) == 0:
                 running.remove(p)
-
-
-MESSAGES = 88 * GROUPS
+    for c in swap:
+        c.wait_send()
+
+
+MESSAGES = 84 * GROUPS + BL
 
 
 def per_device(direct, reflection, onset_plus, onset_minus):
@@ -529,24 +547,25 @@
         in_specs=[vmem] * 8,
         out_specs=(vmem, vmem),
         scratch_shapes=[
-            pltpu.VMEM((BL, 2 * SRC, RCV), bf16),
-            pltpu.VMEM((BL, 2 * SRC, RCV), bf16),
-            pltpu.VMEM((BL, RCV, 2 * SRC), bf16),
-            pltpu.VMEM((BL, RCV, 2 * SRC), bf16),
+            pltpu.VMEM((BL, 2, SRC, HALF), f32),
+            pltpu.VMEM((BL, 4 * SRC, HALF), bf16),
+            pltpu.VMEM((BL, 4 * SRC, HALF), bf16),
+            pltpu.VMEM((BL, HALF, 4 * SRC), bf16),
+            pltpu.VMEM((BL, HALF, 4 * SRC), bf16),
             pltpu.VMEM((2, ST * SH, FP, LN), f32),
             pltpu.VMEM((GROUPS, ST, WIDE), f32),
             pltpu.VMEM((GROUPS, NX, PR, LN), f32),
-            pltpu.VMEM((GROUPS, 6, NX, PR, LN), f32),
-            pltpu.VMEM((GROUPS, 6, NX, PR, LN), f32),
-            pltpu.VMEM((GROUPS, 2, NX, PR, LN), f32),
-            pltpu.VMEM((GROUPS, 2, NX, PR, LN), f32),
-            pltpu.VMEM((GROUPS, 6, NX, PR, LN), f32),
-            pltpu.VMEM((GROUPS, BL, NS * ST, LN), f32),
-            pltpu.VMEM((GROUPS, BL, NR * ST, LN), f32),
-            pltpu.VMEM((GROUPS, 2, BL, ST, LN), f32),
-            pltpu.VMEM((GROUPS, BL, NR * ST, LN), f32),
-            pltpu.VMEM((GROUPS, BL, NS * ST, LN), f32),
-            pltpu.VMEM((GROUPS, 12, BL, ST, LN), f32),
+            pltpu.VMEM((GROUPS, 5, NX, PR, LN), f32),
+            pltpu.VMEM((GROUPS, 5, NX, PR, LN), f32),
+            pltpu.VMEM((GROUPS, 4, NX, PR, LN), f32),
+            pltpu.VMEM((GROUPS, 4, NX, PR, LN), f32),
+            pltpu.VMEM((GROUPS, 5, NX, PR, LN), f32),
+            pltpu.VMEM((GROUPS, BL, NZ * ST, LN), f32),
+            pltpu.VMEM((GROUPS, BL, NY * ST, LN), f32),
+            pltpu.VMEM((GROUPS, 4, BL, ST, LN), f32),
+            pltpu.VMEM((GROUPS, BL, NY * ST, LN), f32),
+            pltpu.VMEM((GROUPS, BL, NZ * ST, LN), f32),
+            pltpu.VMEM((GROUPS, 4, BL, ST, LN), f32),
             pltpu.SemaphoreType.DMA((MESSAGES,)),
             pltpu.SemaphoreType.DMA((MESSAGES,)),
         ],

time: 140 us -> 127 us (0.907)
  Pallas kernels: 133 us -> 121 us
    pallas_call x1, Pallas kernels: 133 us -> 121 us  [per_device(): pl.pallas_call(kernel, out_shape=(traces, traces), in_specs=[vmem] * 8, o...]
where the time goes in v4:
time: 127 us; the launch traced here: 126 us
  Pallas kernels  121 us (95%)
  local copies, waits for them, and re-layouts  4.63 us (4%)
    pallas_call x1, Pallas kernels, per_device(): pl.pallas_call(kernel, out_shape=(traces, traces), in_specs=[vmem] * 8, o...  121 us
    unnamed x4, local copies, waits for them, and re-layouts  4.63 us

profile of v4, /device:TPU:16, one launch (start us, length us, event | category | flops | bytes accessed | tf_op | source)
XLA Modules:
  0.0 125.9 jit_solution(15813550717434203454)
XLA Ops:
  0.6 120.6 %shard_map.95 = (f32[32,16,1024]{2,1,0:T(8,128)}, f32[32,16,1024]{2,1,0:T(8,128)}) custom-call(f32[32,16,1024]{2,1,0:T(8,128)} %direct.1, f32[2,5,128,512]{3,2,1,0:T(8,128)} %refl.1, s32[16,32]{1,0:T(8,128)} %bitcast.2, s32[16,32]{1,0:T(8,128)} %bitcast.3, bf16[2,1024,128]{2,1,0:T(8,128)(2,1)} %constant.8.clone.into, bf16[128,640]{1,0:T(8,128)(2,1)} %constant.9.clone.spread, ...), custom_call_target="tpu_custom_call" | custom-call | tf_op jit(solution)/shard_map/pallas_call | solution.py:544
  121.3 0.0 copy-start
  121.3 3.3 %copy.12 = f32[32,16,1024]{2,1,0:T(8,128)} copy(f32[32,16,1024]{2,1,0:T(8,128)} %get-tuple-element.4) | data formatting | bytes 4194304
  124.6 0.0 copy-done
  124.6 1.3 %copy.13 = f32[32,16,1024]{2,1,0:T(8,128)} copy(f32[32,16,1024]{2,1,0:T(8,128)S(1)} %copy-done) | data formatting | bytes 4194304
Async XLA Ops:
  121.3 3.3 %copy-start = (f32[32,16,1024]{2,1,0:T(8,128)S(1)}, f32[32,16,1024]{2,1,0:T(8,128)}, u32[]{:S(2)}) copy-start(f32[32,16,1024]{2,1,0:T(8,128)} %get-tuple-element.5) | copy-start | bytes 6291460

commit v5 on v4

--- a/solution.py
+++ b/solution.py
@@ -156,8 +156,8 @@
 
 
 def kernel(
-    direct, refl, on_plus, on_minus, into, spread, collect, back,
-    out_plus, out_minus,
+    direct_in, refl_in, on_plus, on_minus, into_in, spread_in, collect_in, back_in,
+    out_plus, out_minus, direct, refl, into, spread, collect, back, local_sem,
     r_land, r_high, r_low, t_high, t_low, onset, spec, piece, piece_sum, land_g, land_r, land_f, land_s,
     xs, y, r4a, cs, h, rs, send_sem, recv_sem,
 ):
@@ -188,6 +188,17 @@
     for peer in peers:
         pl.semaphore_signal(barrier, inc=1, device_id=peer, device_id_type=MESH)
 
+    def lanes_of(on):
+        return pl.ds(pl.multiple_of(on * HALF, HALF), HALF)
+
+    loads = [(into_in, into), (spread_in, spread), (direct_in, direct), (collect_in, collect)]
+    loads += [(back_in, back), (refl_in.at[:, :, :, lanes_of(line)], refl)]
+    loads = [
+        pltpu.make_async_copy(a, b, local_sem.at[n]) for n, (a, b) in enumerate(loads)
+    ]
+    for c in loads:
+        c.start()
+
     names = {}
 
     def copy(name, source, target, device):
@@ -207,16 +218,13 @@
         block = (1 - high_y if dh else high_y) * 2 + (1 - core if dc else core)
         return pl.ds(pl.multiple_of((dl * NR + block) * ST, ST), ST)
 
-    def lanes_of(on):
-        return pl.ds(pl.multiple_of(on * HALF, HALF), HALF)
-
     swap = [
-        copy(("r", j), refl.at[:, j, :, lanes_of(other)], r_land.at[j], at_rcv(1, 0, 0))
+        copy(("r", j), refl_in.at[:, j, :, lanes_of(other)], r_land.at[j], at_rcv(1, 0, 0))
         for j in range(BL)
     ]
 
     def prepare(j):
-        both = (refl[:, j, :, lanes_of(line)], r_land[j])
+        both = (refl[:, j], r_land[j])
         block = jnp.concatenate(
             [
                 b[c, (k * SH + s) * ST : (k * SH + s + 1) * ST]
@@ -301,6 +309,9 @@
             spec[grp, at] = to_spectrum(load(direct, grp, i, NT), into, spread)
             return 0
 
+        if grp == 0:
+            for c in loads[:3]:
+                c.wait()
         lax.fori_loop(0, ST // STEP, spectrum_of, 0, unroll=True)
         if grp == 0:
             pl.semaphore_wait(barrier, len(peers))
@@ -339,6 +350,8 @@
 
             if it == 0 and grp == GROUPS - 1:
                 prepare_onsets()
+                for c in loads[3:]:
+                    c.wait()
             yield
             for n, w, way in ((3, 0, 1), (4, 1, -1)):
                 at = arrive(n)
@@ -539,14 +552,22 @@
 
 def per_device(direct, reflection, onset_plus, onset_minus):
     vmem = pl.BlockSpec(memory_space=pltpu.VMEM)
+    hbm = pl.BlockSpec(memory_space=pl.ANY)
     f32, bf16 = jnp.float32, jnp.bfloat16
-    traces = jax.ShapeDtypeStruct((ST * SH, FP, NT), f32)
+    traces = pltpu.VMEM((ST * SH, FP, NT), f32)
     return pl.pallas_call(
         kernel,
         out_shape=(traces, traces),
-        in_specs=[vmem] * 8,
+        in_specs=[hbm, hbm, vmem, vmem, hbm, hbm, hbm, hbm],
         out_specs=(vmem, vmem),
         scratch_shapes=[
+            pltpu.VMEM((ST * SH, FP, NT), f32),
+            pltpu.VMEM((2, BL, SRC, HALF), f32),
+            pltpu.VMEM((2, NT, LN), bf16),
+            pltpu.VMEM((LN, WIDE), bf16),
+            pltpu.VMEM((2, WIDE, LN), bf16),
+            pltpu.VMEM((LN, NT), bf16),
+            pltpu.SemaphoreType.DMA((6 + 2 * GROUPS,)),
             pltpu.VMEM((BL, 2, SRC, HALF), f32),
             pltpu.VMEM((BL, 4 * SRC, HALF), bf16),
             pltpu.VMEM((BL, 4 * SRC, HALF), bf16),
@@ -570,7 +591,7 @@
             pltpu.SemaphoreType.DMA((MESSAGES,)),
         ],
         compiler_params=pltpu.CompilerParams(
-            collective_id=0, has_side_effects=True, vmem_limit_bytes=56 * 1024 * 1024
+            collective_id=0, has_side_effects=True, vmem_limit_bytes=58 * 1024 * 1024
         ),
     )(direct, reflection, onset_plus.T, onset_minus.T, *[jnp.asarray(a) for a in tables()])
 

time: 127 us -> 122 us (0.961)
  Pallas kernels: 121 us -> 117 us
  local copies, waits for them, and re-layouts: 4.63 us -> 2.64 us
    pallas_call x1, Pallas kernels: 121 us -> 117 us  [per_device(): pl.pallas_call(kernel, out_shape=(traces, traces), in_specs=[hbm, hbm, vm...]
    unnamed x4 -> x2, local copies, waits for them, and re-layouts: 4.63 us -> 2.64 us
where the time goes in v5:
time: 122 us; the launch traced here: 121 us
  Pallas kernels  117 us (96%)
  local copies, waits for them, and re-layouts  2.64 us (2%)
    pallas_call x1, Pallas kernels, per_device(): pl.pallas_call(kernel, out_shape=(traces, traces), in_specs=[hbm, hbm, vm...  117 us
    unnamed x2, local copies, waits for them, and re-layouts  2.64 us

profile of v5, /device:TPU:16, one launch (start us, length us, event | category | flops | bytes accessed | tf_op | source)
XLA Modules:
  0.0 120.6 jit_solution(3584175563207000959)
XLA Ops:
  0.6 117.3 %shard_map.95 = (f32[32,16,1024]{2,1,0:T(8,128)S(1)}, f32[32,16,1024]{2,1,0:T(8,128)S(1)}) custom-call(f32[32,16,1024]{2,1,0:T(8,128)} %direct_in.1, f32[2,5,128,512]{3,2,1,0:T(8,128)} %refl_in.1, s32[16,32]{1,0:T(8,128)} %bitcast.2, s32[16,32]{1,0:T(8,128)} %bitcast.3, bf16[2,1024,128]{2,1,0:T(8,128)(2,1)} %constant.8.clone.into_in, ...), custom_call_target="tpu_custom_call" | custom-call | tf_op jit(solution)/shard_map/pallas_call | solution.py:558
  118.0 1.3 %copy.12 = f32[32,16,1024]{2,1,0:T(8,128)} copy(f32[32,16,1024]{2,1,0:T(8,128)S(1)} %get-tuple-element.2) | data formatting | bytes 4194304
  119.3 1.3 %copy.13 = f32[32,16,1024]{2,1,0:T(8,128)} copy(f32[32,16,1024]{2,1,0:T(8,128)S(1)} %get-tuple-element.3) | data formatting | bytes 4194304

commit v6 on v5

--- a/solution.py
+++ b/solution.py
@@ -315,7 +315,7 @@
         lax.fori_loop(0, ST // STEP, spectrum_of, 0, unroll=True)
         if grp == 0:
             pl.semaphore_wait(barrier, len(peers))
-            for c in swap:
+            for c in swap[:2]:
                 c.start()
 
         for it in range(ITERS):
@@ -357,29 +357,36 @@
                 at = arrive(n)
                 forward_to(("g3", n), at, way)
                 forward_to(("g4", n), rows_at(-2 * way, w), 2 * way)
+            if it == 0 and grp == 0:
+                for c in swap[2:]:
+                    c.start()
             for n in (1, 2, 0):
                 arrive(n)
             yield
             for c in late:
                 c.wait_recv()
-            for c in sent:
-                c.wait_send()
-
-            def forward(j, _):
-                x_high, x_low = halves(unfold(xs[grp, j]))
+            owed = list(sent)
+
+            def forward(j, g_at):
+                x_high, x_low = halves(unfold(xs[g_at, j]))
                 both = mm(r_high[j], jnp.concatenate([x_high, x_low], axis=1))
                 g = fold(both[:, :LN] + both[:, LN:] + mm(r_low[j], x_high))
                 n = 2 * SRC // SH
                 real = is_real((n, LN))
                 turned = swap_parts(g[n:], real)
-                y[grp, j] = g[:n] + jnp.where(real, -turned, turned)
+                y[g_at, j] = g[:n] + jnp.where(real, -turned, turned)
                 return 0
 
+            if it == 0:
+                yield
             for j in range(BL):
-                if it == 0 and grp == 0:
+                if it:
+                    forward(j, grp)
+                elif grp == 0:
                     swap[j].wait_recv()
                     prepare(j)
-                forward(j, 0)
+                    for g_at in range(GROUPS):
+                        forward(j, g_at)
 
             order = (2, 3, 1, 0)
             pair = {
@@ -407,8 +414,7 @@
             yield
             for c in stage:
                 c.wait_recv()
-            for c in list(pair.values()) + stage:
-                c.wait_send()
+            owed += list(pair.values()) + stage
             take_spec(
                 grp,
                 [
@@ -426,6 +432,9 @@
 
             lax.fori_loop(0, ST // STEP, up, 0, unroll=True)
 
+            for c in owed:
+                c.wait_send()
+            owed = []
             pack_spec(grp)
             stage = {}
             for n in order:
@@ -452,8 +461,7 @@
             yield
             for c in pair:
                 c.wait_recv()
-            for c in pair + [c for n in order for c in stage[n]]:
-                c.wait_send()
+            owed += pair + [c for n in order for c in stage[n]]
 
             def adjoint(j, _):
                 block = cs[grp, j]
@@ -469,6 +477,7 @@
                 adjoint(j, 0)
 
             sent = []
+            owed_now, owed = owed, []
             stage = [[], []]
 
             def part_to(name, w, slot, dist, dz, part=None):
@@ -499,6 +508,8 @@
             def bins_of(total):
                 return [total[j] for j in range(BL)]
 
+            for c in owed_now:
+                c.wait_send()
             finish(1, [h[grp, j, rows_at(1)] for j in range(BL)])
             finish(2, [h[grp, j, rows_at(-1)] for j in range(BL)])
             finish(0, [h[grp, j, rows_at(0)] for j in range(BL)])
@@ -516,8 +527,6 @@
             for n in range(5):
                 for c in last[n]:
                     c.wait_recv()
-            for c in sent:
-                c.wait_send()
             pieces = []
             for q in range(NX):
                 total = land_s[grp, 0, q]
@@ -537,6 +546,8 @@
                 return 0
 
             lax.fori_loop(0, ST // STEP, down, 0, unroll=True)
+            for c in sent:
+                c.wait_send()
 
     running = [program(grp) for grp in range(GROUPS)]
     while running:

time: 122 us -> 121 us (level)
  no operation moved by 1% of the time
where the time goes in v6:
time: 121 us; the launch traced here: 120 us
  Pallas kernels  117 us (97%)
  local copies, waits for them, and re-layouts  2.64 us (2%)
    pallas_call x1, Pallas kernels, per_device(): pl.pallas_call(kernel, out_shape=(traces, traces), in_specs=[hbm, hbm, vm...  117 us
    unnamed x2, local copies, waits for them, and re-layouts  2.64 us

profile of v6, /device:TPU:16, one launch (start us, length us, event | category | flops | bytes accessed | tf_op | source)
XLA Modules:
  0.0 119.9 jit_solution(13400117743817321591)
XLA Ops:
  0.6 116.6 %shard_map.95 = (f32[32,16,1024]{2,1,0:T(8,128)S(1)}, f32[32,16,1024]{2,1,0:T(8,128)S(1)}) custom-call(f32[32,16,1024]{2,1,0:T(8,128)} %direct_in.1, f32[2,5,128,512]{3,2,1,0:T(8,128)} %refl_in.1, s32[16,32]{1,0:T(8,128)} %bitcast.2, s32[16,32]{1,0:T(8,128)} %bitcast.3, bf16[2,1024,128]{2,1,0:T(8,128)(2,1)} %constant.8.clone.into_in, ...), custom_call_target="tpu_custom_call" | custom-call | tf_op jit(solution)/shard_map/pallas_call | solution.py:569
  117.2 1.3 %copy.12 = f32[32,16,1024]{2,1,0:T(8,128)} copy(f32[32,16,1024]{2,1,0:T(8,128)S(1)} %get-tuple-element.2) | data formatting | bytes 4194304
  118.6 1.3 %copy.13 = f32[32,16,1024]{2,1,0:T(8,128)} copy(f32[32,16,1024]{2,1,0:T(8,128)S(1)} %get-tuple-element.3) | data formatting | bytes 4194304
